TPU v7x, 256 devices: a whole 4x4x8 slice. The times are simulated.
256 devices in a mesh: dp: 16 (over x, y), ctx: 16 (over z, core).
Axes of the slice: x: 4, y: 4, z: 8, core: 2. Of those that a mesh axis runs over, the one named last changes fastest.
Arguments:
- queries: bfloat16 [32768, 4096], P(('dp', 'ctx')), parts along dimension 0, may hold values from -180 to 180
- key_states: bfloat16 [32768, 512], P(('dp', 'ctx')), parts along dimension 0, may hold values from -5 to 5
- value_states: bfloat16 [32768, 512], P(('dp', 'ctx')), parts along dimension 0, may hold values from -6 to 6
- grad_output: bfloat16 [32768, 4096], P(('dp', 'ctx')), parts along dimension 0, may hold values from -6 to 6
- doc_ids: int32 [32768], P('dp'), parts along dimension 0, may hold values from 0 to 3, never falling along the last dimension, each value on 1 to 1024 neighbouring positions
Outputs:
- query_grad: bfloat16 [32768, 4096], P(('dp', 'ctx')), parts along dimension 0
- key_grad: bfloat16 [32768, 512], P(('dp', 'ctx')), parts along dimension 0
- value_grad: bfloat16 [32768, 512], P(('dp', 'ctx')), parts along dimension 0
There are 16 independent parts, one for each index of `dp`. A program takes and returns all parts, laid end to end along the dimension named above; each array names one. Nothing has to cross between parts.
Inputs may be any that keep to these rules, and one draw needn't show every extreme that they name: `doc_ids`: never falls along positions; each document holds 1 to 1024 positions and one holds exactly 1024.
All inputs are finite; a program needn't handle non-finite values.
Results may differ from a plain program's by a relative error of at most 0.029.
Values may be sent and summed in bfloat16 or wider, within the bound.
No kernel may reach another device: no remote copies, remote signals or barrier semaphores. Data moves between devices by JAX's collectives and lax.ppermute only.
A program may use at most 128 MiB of HBM per device.

v0:
```python
import functools

import jax
import jax.numpy as jnp
from jax import lax
from jax.experimental import pallas as pl
from jax.experimental.pallas import tpu as pltpu
from jax.sharding import PartitionSpec as P

DH = 128
GROUP = 8
SCALE = DH ** (-0.5)
FACTOR = SCALE * 1.4426950408889634
NEG = -1e30
LOW = -1e29
NZ = 8
BLK = 128
NB = 16
LANES = GROUP * BLK
MIB = 1024 * 1024
BF16 = jnp.bfloat16
F32 = jnp.float32

NT = (((1,), (1,)), ((), ()))
NN = (((1,), (0,)), ((), ()))
TN = (((0,), (0,)), ((), ()))


def dot(a, b, dims):
    return lax.dot_general(a, b, dims, preferred_element_type=F32)


def chip(z, offset):
    return lax.rem(z + offset + NZ, NZ)


def aligned(index, size):
    return pl.multiple_of(index * size, size)


def query_rows(doc_ref, info, qrow):
    core, z = info[0], info[1]
    doc = doc_ref[...]
    starts = [jnp.sum((doc < d).astype(F32)).astype(jnp.int32) for d in (1, 2, 3)]
    lane = lax.broadcasted_iota(jnp.int32, (1, BLK), 1)
    for x in range(2):
        block = z if x == 0 else NB - 1 - z
        flip = core if x == 0 else 1 - core
        rot = jnp.where(flip == 1, lax.rem(lane + 64, BLK), lane)
        doc_row = doc_ref[pl.ds(block, 1), :]
        doc_row = jnp.where(flip == 1, pltpu.roll(doc_row, 64, 1), doc_row)
        start = jnp.where(
            doc_row == 0, 0,
            jnp.where(doc_row == 1, starts[0], jnp.where(doc_row == 2, starts[1], starts[2])),
        )
        qrow[x, 0:1, :] = block * BLK + rot
        qrow[x, 1:2, :] = start
        info[2 + x] = lax.div(jnp.min(start), BLK)


def for_tiles(info, qrow, s, body):
    core, z = info[0], info[1]

    def step(t, unused):
        combo, g = lax.div(t, 2), lax.rem(t, 2)
        x, y = jnp.minimum(combo, 1), lax.div(combo, 2)
        b = jnp.where(y == 0, s, NB - 1 - s)
        qb = jnp.where(x == 0, z, NB - 1 - z)

        @pl.when((b <= qb) & (b >= info[2 + x]))
        def _():
            flip = jnp.where(y == 0, core, 1 - core)
            row = lax.broadcasted_iota(jnp.int32, (BLK, 1), 0)
            pos_k = b * BLK + jnp.where(flip == 1, lax.rem(row + 64, BLK), row)
            seen = (pos_k <= qrow[x, 0:1, :]) & (pos_k >= qrow[x, 1:2, :])
            bias = jnp.where(seen, 0.0, NEG)
            body(t, x, y, g, jnp.concatenate([bias] * GROUP, axis=1))

        return 0

    lax.fori_loop(0, 6, step, 0)


def stat_tiles(info, qrow, qst, dst, chunk, s, state):
    k_ref, k_col, v_ref, v_col = chunk

    def body(t, x, y, g, bias):
        i = 2 * x + g
        rows = aligned(y, BLK)
        k = k_ref[pl.ds(rows, BLK), pl.ds(pl.multiple_of(k_col + g * DH, DH), DH)]
        v = v_ref[pl.ds(rows, BLK), pl.ds(pl.multiple_of(v_col + g * DH, DH), DH)]
        score = dot(k, qst[i], NT) * FACTOR + bias
        old = state[i, 0:1, :]
        new = jnp.maximum(old, jnp.max(score, axis=0, keepdims=True))
        p = jnp.exp2(score - new)
        grad = dot(v, dst[i], NT)
        alpha = jnp.exp2(old - new)
        state[i, 0:1, :] = new
        state[i, 1:2, :] = state[i, 1:2, :] * alpha + jnp.sum(p, axis=0, keepdims=True)
        state[i, 2:3, :] = state[i, 2:3, :] * alpha + jnp.sum(p * grad, axis=0, keepdims=True)

    for_tiles(info, qrow, s, body)


def grad_tiles(info, qrow, qst, dst, chunk, s, final, acc, dqt):
    k_ref, k_col, v_ref, v_col = chunk
    acc[...] = jnp.zeros_like(acc)

    def body(t, x, y, g, bias):
        i = 2 * x + g
        rows = aligned(y, BLK)
        k = k_ref[pl.ds(rows, BLK), pl.ds(pl.multiple_of(k_col + g * DH, DH), DH)]
        v = v_ref[pl.ds(rows, BLK), pl.ds(pl.multiple_of(v_col + g * DH, DH), DH)]
        w = jnp.exp2(dot(k, qst[i], NT) * FACTOR + bias - final[i, 0:1, :])
        ds = (w * (dot(v, dst[i], NT) - final[i, 1:2, :])).astype(BF16)
        acc[pl.ds(rows, BLK), pl.ds(aligned(g, DH), DH)] += dot(ds, qst[i], NN)
        acc[pl.ds(rows, BLK), pl.ds(pl.multiple_of(256 + g * DH, DH), DH)] += dot(
            w.astype(BF16), dst[i], NN
        )
        dqt[i] += dot(k, ds, TN)

    for_tiles(info, qrow, s, body)


def write_terms(acc, key_out, key_col, value_out, value_col):
    key_out[:, key_col:key_col + 256] = (acc[:, :256] * SCALE).astype(BF16)
    value_out[:, value_col:value_col + 256] = acc[:, 256:].astype(BF16)


def whole(ref):
    return (ref, 0, ref, 256)


def open_kernel(
    place, doc_ref, q_own, do_own, q_par, do_par, own, info, qrow, qst, dst, state, rows_in, sem
):
    info[0] = place[0]
    info[1] = place[1]
    low = aligned(place[0], 2048)
    copies = [
        pltpu.make_async_copy(source.at[:, pl.ds(low, 2048)], rows_in.at[i], sem.at[i])
        for i, source in enumerate((q_own, do_own, q_par, do_par))
    ]
    for one in copies:
        one.start()
    query_rows(doc_ref, info, qrow)
    for i, one in enumerate(copies):
        one.wait()
        out, part = (qst, dst)[i % 2], i // 2
        for x in range(2):
            for g in range(2):
                for h in range(GROUP):
                    cols = slice((g * GROUP + h) * DH, (g * GROUP + h + 1) * DH)
                    rows = slice(h * BLK + part * 64, h * BLK + part * 64 + 64)
                    out[2 * x + g, rows, :] = rows_in[i, x * 64:x * 64 + 64, cols]
    for i in range(4):
        state[i, 0:1, :] = jnp.full((1, LANES), LOW, F32)
        state[i, 1:3, :] = jnp.zeros((2, LANES), F32)
    stat_tiles(info, qrow, qst, dst, whole(own), info[1], state)


def stat_kernel(distance, info, qrow, qst, dst, up, down, state_in, state):
    state[...] = state_in[...]
    stat_tiles(info, qrow, qst, dst, whole(up), chip(info[1], -distance), state)
    stat_tiles(info, qrow, qst, dst, whole(down), chip(info[1], distance), state)


def far_kernel(
    info, qrow, qst, dst, far_k, far_v, state_in, final, tk, tv, ds_out,
    state, acc, probs, grads, maxes,
):
    state[...] = state_in[...]
    acc[...] = jnp.zeros_like(acc)
    s = chip(info[1], 4)

    def first(t, x, y, g, bias):
        i = 2 * x + g
        rows, cols = aligned(y, BLK), aligned(g, DH)
        score = dot(far_k[pl.ds(rows, BLK), pl.ds(cols, DH)], qst[i], NT) * FACTOR + bias
        old = state[i, 0:1, :]
        new = jnp.maximum(old, jnp.max(score, axis=0, keepdims=True))
        p = jnp.exp2(score - new)
        grad = dot(far_v[pl.ds(rows, BLK), pl.ds(cols, DH)], dst[i], NT)
        alpha = jnp.exp2(old - new)
        probs[t] = p
        grads[t] = grad
        maxes[t, 0:1, :] = new
        state[i, 0:1, :] = new
        state[i, 1:2, :] = state[i, 1:2, :] * alpha + jnp.sum(p, axis=0, keepdims=True)
        state[i, 2:3, :] = state[i, 2:3, :] * alpha + jnp.sum(p * grad, axis=0, keepdims=True)

    for_tiles(info, qrow, s, first)
    for i in range(4):
        total = state[i, 1:2, :]
        final[i, 0:1, :] = state[i, 0:1, :] + jnp.log2(total)
        final[i, 1:2, :] = state[i, 2:3, :] / total

    def second(t, x, y, g, bias):
        i = 2 * x + g
        rows, cols = aligned(y, BLK), aligned(g, DH)
        w = probs[t] * jnp.exp2(maxes[t, 0:1, :] - final[i, 0:1, :])
        ds = (w * (grads[t] - final[i, 1:2, :])).astype(BF16)
        ds_out[t] = ds
        acc[pl.ds(rows, BLK), pl.ds(cols, DH)] += dot(ds, qst[i], NN)
        acc[pl.ds(rows, BLK), pl.ds(pl.multiple_of(256 + g * DH, DH), DH)] += dot(
            w.astype(BF16), dst[i], NN
        )

    for_tiles(info, qrow, s, second)
    write_terms(acc, tk, 0, tv, 0)


def far_query(info, qrow, far_k, ds_in, dqt):
    def body(t, x, y, g, bias):
        k = far_k[pl.ds(aligned(y, BLK), BLK), pl.ds(aligned(g, DH), DH)]
        dqt[2 * x + g] += dot(k, ds_in[t], TN)

    for_tiles(info, qrow, chip(info[1], 4), body)


def third_kernel(info, qrow, qst, dst, up, down, final, tu, td, dqt, acc):
    dqt[...] = jnp.zeros_like(dqt)
    grad_pair(3, info, qrow, qst, dst, up, down, final, tu, td, dqt, acc)


def second_kernel(
    info, qrow, qst, dst, up, down, final, dqt_in, far_k, ds_in, tu, td, dqt, acc
):
    dqt[...] = dqt_in[...]
    grad_pair(2, info, qrow, qst, dst, up, down, final, tu, td, dqt, acc)
    far_query(info, qrow, far_k, ds_in, dqt)


def first_kernel(info, qrow, qst, dst, up, down, final, dqt_in, tu, td, dqt, acc):
    dqt[...] = dqt_in[...]
    grad_pair(1, info, qrow, qst, dst, up, down, final, tu, td, dqt, acc)


def grad_pair(distance, info, qrow, qst, dst, up, down, final, tu, td, dqt, acc):
    for chunk, out, offset in ((up, td, -distance), (down, tu, distance)):
        s = chip(info[1], offset)
        grad_tiles(info, qrow, qst, dst, whole(chunk), s, final, acc, dqt)
        write_terms(acc, out, 0, out, 256)


def close_kernel(info, qrow, qst, dst, own, final, dqt_in, t0, dq_own, dq_par, dqt, acc):
    dqt[...] = dqt_in[...]
    grad_tiles(info, qrow, qst, dst, whole(own), info[1], final, acc, dqt)
    write_terms(acc, t0, 0, t0, 256)
    for x in range(2):
        for g in range(2):
            for h in range(GROUP):
                part = dqt[2 * x + g, :, h * BLK:(h + 1) * BLK] * SCALE
                out = jnp.transpose(part).astype(BF16)
                cols = slice((g * GROUP + h) * DH, (g * GROUP + h + 1) * DH)
                dq_own[x * 64:x * 64 + 64, cols] = out[:64]
                dq_par[x * 64:x * 64 + 64, cols] = out[64:]


def assemble_kernel(place, mine, got, up, down, own):
    for part, source in ((0, mine), (64, got)):
        for out in (up, down, own):
            out[part:part + 64, :] = source[:64, :]
            out[BLK + part:BLK + part + 64, :] = source[64:, :]


def add_kernel(place, tu, td, up, down, up_out, down_out):
    width = up.shape[1]
    if width < 512:
        up_out[:, width:] = tu[:, width:]
        down_out[:, :512 - width] = td[:, :512 - width]
    cols = slice(0, width)
    up_out[:, cols] = (tu[:, cols].astype(F32) + up[...].astype(F32)).astype(BF16)
    cols = slice(512 - width, 512)
    down_out[:, cols] = (td[:, cols].astype(F32) + down[...].astype(F32)).astype(BF16)


def last_kernel(place, total, back, key, value, sem):
    core = place[0]
    mine, other = aligned(core, 256), aligned(1 - core, 256)
    copies = []
    for out, low in ((key, 0), (value, 256)):
        cols = pl.ds(low, 256)
        for source, target in (
            (total.at[pl.ds(0, 64), cols], out.at[pl.ds(0, 64), pl.ds(mine, 256)]),
            (total.at[pl.ds(128, 64), cols], out.at[pl.ds(64, 64), pl.ds(mine, 256)]),
            (back.at[:, cols], out.at[:, pl.ds(other, 256)]),
        ):
            copies.append(pltpu.make_async_copy(source, target, sem.at[len(copies)]))
            copies[-1].start()
    for one in copies:
        one.wait()


SMEM_SPEC = pl.BlockSpec(memory_space=pltpu.SMEM)
VMEM_SPEC = pl.BlockSpec(memory_space=pltpu.VMEM)
ANY_SPEC = pl.BlockSpec(memory_space=pltpu.HBM)


def shape(dims, dtype=BF16):
    return jax.ShapeDtypeStruct(dims, dtype)


INFO = shape((8,), jnp.int32)
QROW = shape((2, 8, BLK), jnp.int32)
STACK = shape((4, LANES, DH))
STATE = shape((4, 8, LANES), F32)
TERM = shape((256, 512))
HALF_TERM = shape((256, 256))
DQT = shape((4, DH, LANES), F32)
DQ = shape((BLK, 2048))


def call(kernel, out, args, scratch=(), cost=3, limit=24, first_out_smem=False, far=(), far_out=False):
    in_specs = [SMEM_SPEC] + [
        ANY_SPEC if i in far else VMEM_SPEC for i in range(1, len(args))
    ]
    specs = [ANY_SPEC if far_out else VMEM_SPEC] * len(out)
    if first_out_smem:
        specs[0] = SMEM_SPEC
    return pl.pallas_call(
        kernel,
        out_shape=tuple(out),
        in_specs=in_specs,
        out_specs=tuple(specs),
        scratch_shapes=list(scratch),
        compiler_params=pltpu.CompilerParams(vmem_limit_bytes=limit * MIB),
        cost_estimate=pl.CostEstimate(flops=cost * 10**9, bytes_accessed=10**6, transcendentals=0),
    )(*args)


SWAP = [(i, i ^ 1) for i in range(2 * NZ)]


def swap(x):
    return lax.ppermute(x, "ctx", SWAP)


def ring(x, step):
    pairs = [(2 * z + c, 2 * ((z + step) % NZ) + c) for z in range(NZ) for c in range(2)]
    return lax.ppermute(x, "ctx", pairs)


def half_of(x, index):
    width = x.shape[1] // 2
    return lax.dynamic_slice_in_dim(x, index * width, width, 1)


def join(mine, other, core):
    return jnp.where(
        core == 0,
        jnp.concatenate([mine, other], axis=1),
        jnp.concatenate([other, mine], axis=1),
    )


def add(a, b):
    return (a.astype(F32) + b.astype(F32)).astype(BF16)


def per_device(queries, key_states, value_states, grad_output, doc_ids):
    index = lax.axis_index("ctx")
    core, z = index % 2, index // 2
    place = jnp.stack([core, z]).astype(jnp.int32)
    doc = doc_ids.reshape(NB, BLK)

    mine = jnp.concatenate([half_of(key_states, core), half_of(value_states, core)], axis=1)
    other = jnp.concatenate([half_of(key_states, 1 - core), half_of(value_states, 1 - core)], axis=1)
    got = swap(other)
    own_up, own_down, own = call(assemble_kernel, [TERM] * 3, [place, mine, got])
    together = lax.optimization_barrier
    q_in, do_in, unused = together((queries, grad_output, got))
    q_par, do_par = swap(q_in), swap(do_in)
    up, down = ring(own_up, 1), ring(own_down, -1)
    info, qrow, qst, dst, state = call(
        open_kernel,
        [INFO, QROW, STACK, STACK, STATE],
        [place, doc, queries, grad_output, q_par, do_par, own],
        [pltpu.VMEM((4, BLK, 2048), BF16), pltpu.SemaphoreType.DMA((4,))],
        first_out_smem=True, far=(2, 3, 4, 5),
    )
    common = [info, qrow, qst, dst]
    ups, downs = [], []
    for k in (1, 2, 3):
        up, down, state = together((up, down, state))
        ups.append(up)
        downs.append(down)
        if k < 3:
            next_up, next_down = ring(up, 1), ring(down, -1)
        else:
            far_up, far_down = together((up[:, :256], down[:, 256:]))
            next_up, next_down = ring(far_up, 1), ring(far_down, -1)
        (state,) = call(
            functools.partial(stat_kernel, k), [STATE], common + [up, down, state]
        )
        up, down = next_up, next_down
    far_k, far_v = up, down
    acc = pltpu.VMEM((256, 512), F32)
    tiles = (6, BLK, LANES)
    final, tk, tv, ds_far = call(
        far_kernel, [STATE, HALF_TERM, HALF_TERM, shape(tiles)], common + [far_k, far_v, state],
        [pltpu.VMEM(STATE.shape, F32), acc, pltpu.VMEM(tiles, F32), pltpu.VMEM(tiles, F32),
         pltpu.VMEM((6, 8, LANES), F32)],
    )
    up, down = ring(tk, 1), ring(tv, -1)
    for k in (3, 2, 1):
        chunks = common + [ups[k - 1], downs[k - 1], final]
        outs = [TERM, TERM, DQT]
        if k == 3:
            tu, td, dqt = call(third_kernel, outs, chunks, [acc], cost=5)
        elif k == 2:
            tu, td, dqt = call(second_kernel, outs, chunks + [dqt, far_k, ds_far], [acc], cost=5)
        else:
            tu, td, dqt = call(first_kernel, outs, chunks + [dqt], [acc], cost=5)
        up, down, tu, td, dqt = together((up, down, tu, td, dqt))
        if k == 3:
            up = jnp.concatenate([add(tu[:, :256], up), tu[:, 256:]], axis=1)
            down = jnp.concatenate([td[:, :256], add(td[:, 256:], down)], axis=1)
        else:
            up, down = add(tu, up), add(td, down)
        up, down = together((up, down))
        up, down = ring(up, 1), ring(down, -1)
    t0, dq_own, dq_par = call(
        close_kernel, [TERM, DQ, DQ], common + [own, final, dqt],
        [pltpu.VMEM(DQT.shape, F32), acc], cost=5,
    )
    dq_got = swap(dq_par)
    total = (t0.astype(F32) + up.astype(F32) + down.astype(F32)).astype(BF16)
    away = jnp.concatenate([total[64:128], total[192:]], axis=0)
    away, dq_own = together((away, dq_own))
    back = swap(away)
    query_grad, total = together((join(dq_own, dq_got, core), total))
    key_grad, value_grad = call(
        last_kernel, [shape((BLK, 512))] * 2, [place, total, back],
        [pltpu.SemaphoreType.DMA((6,))], far_out=True,
    )
    return (query_grad, key_grad, value_grad)


def solution(mesh):
    rows = P(("dp", "ctx"), None)
    return jax.shard_map(
        per_device,
        mesh=mesh,
        in_specs=(rows, rows, rows, rows, P("dp")),
        out_specs=(rows, rows, rows),
        check_vma=False,
    )
```

profile of v0, /device:TPU:23, one launch (start us, length us, event | category | flops | bytes accessed | tf_op | source)
XLA Modules:
  0.0 85.1 jit_solution(4950536052802737297)
XLA Ops:
  4.6 1.7 %collective-permute-start.3 = (bf16[256,512]{1,0:T(8,128)(2,1)S(1)}, bf16[256,512]{1,0:T(8,128)(2,1)S(1)}, u32[]{:S(2)}, u32[]{:S(2)}) collective-permute-start(bf16[256,512]{1,0:T(8,128)(2,1)S(1)} %get-tuple-element.74), channel_id=1, source_target_pairs={{0,2},{1,3},{2,4},{3,5},{4,6},{5,7},{6,8},{7,9},{8,10},{9,11},{10,... | collective-permute-start | bytes 786440 | tf_op jit(solution)/shard_map/ppermute | solution.py:341
  6.3 4.0 %collective-permute-start.4 = (bf16[256,512]{1,0:T(8,128)(2,1)S(1)}, bf16[256,512]{1,0:T(8,128)(2,1)S(1)}, u32[]{:S(2)}, u32[]{:S(2)}) collective-permute-start(bf16[256,512]{1,0:T(8,128)(2,1)S(1)} %get-tuple-element.75), channel_id=1, source_target_pairs={{0,14},{1,15},{2,0},{3,1},{4,2},{5,3},{6,4},{7,5},{8,6},{9,7},{10,... | collective-permute-start | bytes 786440 | tf_op jit(solution)/shard_map/ppermute | solution.py:341
  10.4 3.6 %shard_map.77 = (s32[8]{0:T(128)S(1)}, s32[2,8,128]{2,1,0:T(8,128)S(1)}, bf16[4,1024,128]{2,1,0:T(8,128)(2,1)S(1)}, bf16[4,1024,128]{2,1,0:T(8,128)(2,1)S(1)}, f32[4,8,1024]{2,1,0:T(8,128)S(1)}) custom-call(s32[2]{0:T(128)S(1)} %pad_add_fusion.place, s32[16,128]{1,0:T(8,128)S(1)} %bitcast.3, bf16[128,4096]{1,0:T(8,128)(2,1)S(1)} %copy-done, ...), custom_call_target="tpu_custom_call" | custom-call | flops 3000000000 | bytes 1000000 | tf_op jit(solution)/shard_map/pallas_call | solution.py:321
  14.0 2.7 %collective-permute-done.3.up = bf16[256,512]{1,0:T(8,128)(2,1)S(1)} collective-permute-done((bf16[256,512]{1,0:T(8,128)(2,1)S(1)}, bf16[256,512]{1,0:T(8,128)(2,1)S(1)}, u32[]{:S(2)}, u32[]{:S(2)}) %collective-permute-start.3) | collective-permute-done | bytes 262176 | tf_op jit(solution)/shard_map/ppermute | solution.py:341
  16.7 2.7 %collective-permute-start.6 = (bf16[256,512]{1,0:T(8,128)(2,1)S(1)}, bf16[256,512]{1,0:T(8,128)(2,1)S(1)}, u32[]{:S(2)}, u32[]{:S(2)}) collective-permute-start(bf16[256,512]{1,0:T(8,128)(2,1)S(1)} %collective-permute-done.4.down), channel_id=1, source_target_pairs={{0,14},{1,15},{2,0},{3,1},{4,2},{5,3},{6,4},{7,5},{8,6},{9,7},{10,... | collective-permute-start | bytes 786440 | tf_op jit(solution)/shard_map/ppermute | solution.py:341
  19.3 1.5 %shard_map.78.state_in = f32[4,8,1024]{2,1,0:T(8,128)S(1)} custom-call(s32[8]{0:T(128)S(1)} %get-tuple-element.70.info, s32[2,8,128]{2,1,0:T(8,128)S(1)} %get-tuple-element.71.qrow, bf16[4,1024,128]{2,1,0:T(8,128)(2,1)S(1)} %get-tuple-element.72.qst, bf16[4,1024,128]{2,1,0:T(8,128)(2,1)S(1)} %get-tuple-element.73.dst, ...), custom_call_target="tpu_custom_call" | custom-call | flops 3000000000 | bytes 1000000 | tf_op jit(solution)/shard_map/pallas_call | solution.py:321
  20.9 4.0 %collective-permute-done.5.up = bf16[256,512]{1,0:T(8,128)(2,1)S(1)} collective-permute-done((bf16[256,512]{1,0:T(8,128)(2,1)S(1)}, bf16[256,512]{1,0:T(8,128)(2,1)S(1)}, u32[]{:S(2)}, u32[]{:S(2)}) %collective-permute-start.5) | collective-permute-done | bytes 262176 | tf_op jit(solution)/shard_map/ppermute | solution.py:341
  25.7 1.8 %collective-permute-start.8 = (bf16[256,512]{1,0:T(8,128)(2,1)S(1)}, bf16[256,512]{1,0:T(8,128)(2,1)S(1)}, u32[]{:S(2)}, u32[]{:S(2)}) collective-permute-start(bf16[256,512]{1,0:T(8,128)(2,1)S(1)} %collective-permute-done.6.down), channel_id=1, source_target_pairs={{0,14},{1,15},{2,0},{3,1},{4,2},{5,3},{6,4},{7,5},{8,6},{9,7},{10,... | collective-permute-start | bytes 786440 | tf_op jit(solution)/shard_map/ppermute | solution.py:341
  27.5 1.5 %shard_map.79.state_in = f32[4,8,1024]{2,1,0:T(8,128)S(1)} custom-call(s32[8]{0:T(128)S(1)} %get-tuple-element.70.info, s32[2,8,128]{2,1,0:T(8,128)S(1)} %get-tuple-element.71.qrow, bf16[4,1024,128]{2,1,0:T(8,128)(2,1)S(1)} %get-tuple-element.72.qst, bf16[4,1024,128]{2,1,0:T(8,128)(2,1)S(1)} %get-tuple-element.73.dst, ...), custom_call_target="tpu_custom_call" | custom-call | flops 3000000000 | bytes 1000000 | tf_op jit(solution)/shard_map/pallas_call | solution.py:321
  29.0 3.0 %collective-permute-done.7.up = bf16[256,512]{1,0:T(8,128)(2,1)S(1)} collective-permute-done((bf16[256,512]{1,0:T(8,128)(2,1)S(1)}, bf16[256,512]{1,0:T(8,128)(2,1)S(1)}, u32[]{:S(2)}, u32[]{:S(2)}) %collective-permute-start.7) | collective-permute-done | bytes 262176 | tf_op jit(solution)/shard_map/ppermute | solution.py:341
  32.9 1.9 %collective-permute-start.10 = (bf16[256,256]{1,0:T(8,128)(2,1)S(1)}, bf16[256,256]{1,0:T(8,128)(2,1)S(1)}, u32[]{:S(2)}, u32[]{:S(2)}) collective-permute-start(bf16[256,256]{1,0:T(8,128)(2,1)S(1)} %slice.25), channel_id=1, source_target_pairs={{0,14},{1,15},{2,0},{3,1},{4,2},{5,3},{6,4},{7,5},{8,6},{9,7},{10,... | collective-permute-start | bytes 393224 | tf_op jit(solution)/shard_map/ppermute | solution.py:341
  35.7 1.6 %collective-permute-done.9.far_k = bf16[256,256]{1,0:T(8,128)(2,1)S(1)} collective-permute-done((bf16[256,256]{1,0:T(8,128)(2,1)S(1)}, bf16[256,256]{1,0:T(8,128)(2,1)S(1)}, u32[]{:S(2)}, u32[]{:S(2)}) %collective-permute-start.9) | collective-permute-done | bytes 131104 | tf_op jit(solution)/shard_map/ppermute | solution.py:341
  39.3 1.8 %collective-permute-start.12 = (bf16[256,256]{1,0:T(8,128)(2,1)S(1)}, bf16[256,256]{1,0:T(8,128)(2,1)S(1)}, u32[]{:S(2)}, u32[]{:S(2)}) collective-permute-start(bf16[256,256]{1,0:T(8,128)(2,1)S(1)} %get-tuple-element.90), channel_id=1, source_target_pairs={{0,14},{1,15},{2,0},{3,1},{4,2},{5,3},{6,4},{7,5},{8,6},{9,7},{10,... | collective-permute-start | bytes 393224 | tf_op jit(solution)/shard_map/ppermute | solution.py:341
  43.4 2.3 %collective-permute-done.12 = bf16[256,256]{1,0:T(8,128)(2,1)S(1)} collective-permute-done((bf16[256,256]{1,0:T(8,128)(2,1)S(1)}, bf16[256,256]{1,0:T(8,128)(2,1)S(1)}, u32[]{:S(2)}, u32[]{:S(2)}) %collective-permute-start.12) | collective-permute-done | bytes 131104 | tf_op jit(solution)/shard_map/ppermute | solution.py:341
  45.9 1.9 %collective-permute-start.13 = (bf16[256,512]{1,0:T(8,128)(2,1)S(1)}, bf16[256,512]{1,0:T(8,128)(2,1)S(1)}, u32[]{:S(2)}, u32[]{:S(2)}) collective-permute-start(bf16[256,512]{1,0:T(8,128)(2,1)S(1)} %pad_maximum_fusion), channel_id=1, source_target_pairs={{0,2},{1,3},{2,4},{3,5},{4,6},{5,7},{6,8},{7,9},{8,10},{9,11},{10,... | collective-permute-start | bytes 786440 | tf_op jit(solution)/shard_map/ppermute | solution.py:341
  48.6 2.3 %shard_map.83 = (bf16[256,512]{1,0:T(8,128)(2,1)S(1)}, bf16[256,512]{1,0:T(8,128)(2,1)S(1)}, f32[4,128,1024]{2,1,0:T(8,128)S(1)}) custom-call(s32[8]{0:T(128)S(1)} %get-tuple-element.70.info, s32[2,8,128]{2,1,0:T(8,128)S(1)} %get-tuple-element.71.qrow, bf16[4,1024,128]{2,1,0:T(8,128)(2,1)S(1)} %get-tuple-element.72.qst, ...), custom_call_target="tpu_custom_call" | custom-call | flops 5000000000 | bytes 1000000 | tf_op jit(solution)/shard_map/pallas_call | solution.py:321
  52.4 2.2 %collective-permute-done.14 = bf16[256,512]{1,0:T(8,128)(2,1)S(1)} collective-permute-done((bf16[256,512]{1,0:T(8,128)(2,1)S(1)}, bf16[256,512]{1,0:T(8,128)(2,1)S(1)}, u32[]{:S(2)}, u32[]{:S(2)}) %collective-permute-start.14) | collective-permute-done | bytes 262176 | tf_op jit(solution)/shard_map/ppermute | solution.py:341
  54.7 1.5 %collective-permute-start.15 = (bf16[256,512]{1,0:T(8,128)(2,1)S(1)}, bf16[256,512]{1,0:T(8,128)(2,1)S(1)}, u32[]{:S(2)}, u32[]{:S(2)}) collective-permute-start(bf16[256,512]{1,0:T(8,128)(2,1)S(1)} %add_convert_fusion.4), channel_id=1, source_target_pairs={{0,2},{1,3},{2,4},{3,5},{4,6},{5,7},{6,8},{7,9},{8,10},{9,11},{10,... | collective-permute-start | bytes 786440 | tf_op jit(solution)/shard_map/ppermute | solution.py:341
  57.5 2.2 %shard_map.84 = (bf16[256,512]{1,0:T(8,128)(2,1)S(1)}, bf16[256,512]{1,0:T(8,128)(2,1)S(1)}, f32[4,128,1024]{2,1,0:T(8,128)S(1)}) custom-call(s32[8]{0:T(128)S(1)} %get-tuple-element.70.info, s32[2,8,128]{2,1,0:T(8,128)S(1)} %get-tuple-element.71.qrow, bf16[4,1024,128]{2,1,0:T(8,128)(2,1)S(1)} %get-tuple-element.72.qst, ...), custom_call_target="tpu_custom_call" | custom-call | flops 5000000000 | bytes 1000000 | tf_op jit(solution)/shard_map/pallas_call | solution.py:321
  59.7 1.9 %collective-permute-done.15 = bf16[256,512]{1,0:T(8,128)(2,1)S(1)} collective-permute-done((bf16[256,512]{1,0:T(8,128)(2,1)S(1)}, bf16[256,512]{1,0:T(8,128)(2,1)S(1)}, u32[]{:S(2)}, u32[]{:S(2)}) %collective-permute-start.15) | collective-permute-done | bytes 262176 | tf_op jit(solution)/shard_map/ppermute | solution.py:341
  61.6 1.6 %collective-permute-done.16 = bf16[256,512]{1,0:T(8,128)(2,1)S(1)} collective-permute-done((bf16[256,512]{1,0:T(8,128)(2,1)S(1)}, bf16[256,512]{1,0:T(8,128)(2,1)S(1)}, u32[]{:S(2)}, u32[]{:S(2)}) %collective-permute-start.16) | collective-permute-done | bytes 262176 | tf_op jit(solution)/shard_map/ppermute | solution.py:341
  63.3 1.8 %collective-permute-start.17 = (bf16[256,512]{1,0:T(8,128)(2,1)S(1)}, bf16[256,512]{1,0:T(8,128)(2,1)S(1)}, u32[]{:S(2)}, u32[]{:S(2)}) collective-permute-start(bf16[256,512]{1,0:T(8,128)(2,1)S(1)} %add_convert_fusion.2), channel_id=1, source_target_pairs={{0,2},{1,3},{2,4},{3,5},{4,6},{5,7},{6,8},{7,9},{8,10},{9,11},{10,... | collective-permute-start | bytes 786440 | tf_op jit(solution)/shard_map/ppermute | solution.py:341
  66.1 3.5 %shard_map.85 = (bf16[256,512]{1,0:T(8,128)(2,1)S(1)}, bf16[128,2048]{1,0:T(8,128)(2,1)S(1)}, bf16[128,2048]{1,0:T(8,128)(2,1)S(1)}) custom-call(s32[8]{0:T(128)S(1)} %get-tuple-element.70.info, s32[2,8,128]{2,1,0:T(8,128)S(1)} %get-tuple-element.71.qrow, bf16[4,1024,128]{2,1,0:T(8,128)(2,1)S(1)} %get-tuple-element.72.qst, ...), custom_call_target="tpu_custom_call" | custom-call | flops 5000000000 | bytes 1000000 | tf_op jit(solution)/shard_map/pallas_call | solution.py:321
  69.6 11.3 %collective-permute-start.19 = (bf16[128,2048]{1,0:T(8,128)(2,1)S(1)}, bf16[128,2048]{1,0:T(8,128)(2,1)S(1)}, u32[]{:S(2)}, u32[]{:S(2)}) collective-permute-start(bf16[128,2048]{1,0:T(8,128)(2,1)S(1)} %get-tuple-element.125), channel_id=1, source_target_pairs={{0,1},{1,0},{2,3},{3,2},{4,5},{5,4},{6,7},{7,6},{8,9},{9,8},{10,11... | collective-permute-start | bytes 1572872 | tf_op jit(solution)/shard_map/ppermute | solution.py:336
  (55 shorter events, 19.6 us)
Async XLA Ops:
  1.6 1.7 %collective-permute-start = (bf16[128,512]{1,0:T(8,128)(2,1)S(1)}, bf16[128,512]{1,0:T(8,128)(2,1)S(1)}, u32[]{:S(2)}, u32[]{:S(2)}) collective-permute-start(bf16[128,512]{1,0:T(8,128)(2,1)S(1)} %pad_maximum_fusion.2), channel_id=1, source_target_pairs={{0,1},{1,0},{2,3},{3,2},{4,5},{5,4},{6,7},{7,6},{8,9},{9,8},{10,11... | collective-permute-start | bytes 393224 | tf_op jit(solution)/shard_map/ppermute | solution.py:336
  3.4 7.0 %collective-permute-start.1 = (bf16[128,4096]{1,0:T(8,128)(2,1)}, bf16[128,4096]{1,0:T(8,128)(2,1)S(1)}, u32[]{:S(2)}, u32[]{:S(2)}) collective-permute-start(bf16[128,4096]{1,0:T(8,128)(2,1)} %q_own.1), channel_id=1, source_target_pairs={{0,1},{1,0},{2,3},{3,2},{4,5},{5,4},{6,7},{7,6},{8,9},{9,8},{10,11... | collective-permute-start | bytes 3145736 | tf_op jit(solution)/shard_map/ppermute | solution.py:336
  3.7 6.6 %collective-permute-start.2 = (bf16[128,4096]{1,0:T(8,128)(2,1)}, bf16[128,4096]{1,0:T(8,128)(2,1)S(1)}, u32[]{:S(2)}, u32[]{:S(2)}) collective-permute-start(bf16[128,4096]{1,0:T(8,128)(2,1)} %do_own.1), channel_id=1, source_target_pairs={{0,1},{1,0},{2,3},{3,2},{4,5},{5,4},{6,7},{7,6},{8,9},{9,8},{10,11... | collective-permute-start | bytes 3145736 | tf_op jit(solution)/shard_map/ppermute | solution.py:336
  4.0 6.4 %copy-start = (bf16[128,4096]{1,0:T(8,128)(2,1)S(1)}, bf16[128,4096]{1,0:T(8,128)(2,1)}, u32[]{:S(2)}) copy-start(bf16[128,4096]{1,0:T(8,128)(2,1)} %q_own.1) | copy-start | bytes 3145732
  4.0 6.4 %copy-start.1 = (bf16[128,4096]{1,0:T(8,128)(2,1)S(1)}, bf16[128,4096]{1,0:T(8,128)(2,1)}, u32[]{:S(2)}) copy-start(bf16[128,4096]{1,0:T(8,128)(2,1)} %do_own.1) | copy-start | bytes 3145732
  4.0 6.4 %copy-start.2 = (s32[2048]{0:T(1024)S(1)}, s32[2048]{0:T(1024)}, u32[]{:S(2)}) copy-start(s32[2048]{0:T(1024)} %param.9) | copy-start | bytes 24580
  4.6 12.0 %collective-permute-start.3 = (bf16[256,512]{1,0:T(8,128)(2,1)S(1)}, bf16[256,512]{1,0:T(8,128)(2,1)S(1)}, u32[]{:S(2)}, u32[]{:S(2)}) collective-permute-start(bf16[256,512]{1,0:T(8,128)(2,1)S(1)} %get-tuple-element.74), channel_id=1, source_target_pairs={{0,2},{1,3},{2,4},{3,5},{4,6},{5,7},{6,8},{7,9},{8,10},{9,11},{10,... | collective-permute-start | bytes 786440 | tf_op jit(solution)/shard_map/ppermute | solution.py:341
  6.3 10.3 %collective-permute-start.4 = (bf16[256,512]{1,0:T(8,128)(2,1)S(1)}, bf16[256,512]{1,0:T(8,128)(2,1)S(1)}, u32[]{:S(2)}, u32[]{:S(2)}) collective-permute-start(bf16[256,512]{1,0:T(8,128)(2,1)S(1)} %get-tuple-element.75), channel_id=1, source_target_pairs={{0,14},{1,15},{2,0},{3,1},{4,2},{5,3},{6,4},{7,5},{8,6},{9,7},{10,... | collective-permute-start | bytes 786440 | tf_op jit(solution)/shard_map/ppermute | solution.py:341
  16.7 8.2 %collective-permute-start.5 = (bf16[256,512]{1,0:T(8,128)(2,1)S(1)}, bf16[256,512]{1,0:T(8,128)(2,1)S(1)}, u32[]{:S(2)}, u32[]{:S(2)}) collective-permute-start(bf16[256,512]{1,0:T(8,128)(2,1)S(1)} %collective-permute-done.3.up), channel_id=1, source_target_pairs={{0,2},{1,3},{2,4},{3,5},{4,6},{5,7},{6,8},{7,9},{8,10},{9,11},{10,... | collective-permute-start | bytes 786440 | tf_op jit(solution)/shard_map/ppermute | solution.py:341
  16.7 8.2 %collective-permute-start.6 = (bf16[256,512]{1,0:T(8,128)(2,1)S(1)}, bf16[256,512]{1,0:T(8,128)(2,1)S(1)}, u32[]{:S(2)}, u32[]{:S(2)}) collective-permute-start(bf16[256,512]{1,0:T(8,128)(2,1)S(1)} %collective-permute-done.4.down), channel_id=1, source_target_pairs={{0,14},{1,15},{2,0},{3,1},{4,2},{5,3},{6,4},{7,5},{8,6},{9,7},{10,... | collective-permute-start | bytes 786440 | tf_op jit(solution)/shard_map/ppermute | solution.py:341
  24.8 7.2 %collective-permute-start.7 = (bf16[256,512]{1,0:T(8,128)(2,1)S(1)}, bf16[256,512]{1,0:T(8,128)(2,1)S(1)}, u32[]{:S(2)}, u32[]{:S(2)}) collective-permute-start(bf16[256,512]{1,0:T(8,128)(2,1)S(1)} %collective-permute-done.5.up), channel_id=1, source_target_pairs={{0,2},{1,3},{2,4},{3,5},{4,6},{5,7},{6,8},{7,9},{8,10},{9,11},{10,... | collective-permute-start | bytes 786440 | tf_op jit(solution)/shard_map/ppermute | solution.py:341
  25.7 6.4 %collective-permute-start.8 = (bf16[256,512]{1,0:T(8,128)(2,1)S(1)}, bf16[256,512]{1,0:T(8,128)(2,1)S(1)}, u32[]{:S(2)}, u32[]{:S(2)}) collective-permute-start(bf16[256,512]{1,0:T(8,128)(2,1)S(1)} %collective-permute-done.6.down), channel_id=1, source_target_pairs={{0,14},{1,15},{2,0},{3,1},{4,2},{5,3},{6,4},{7,5},{8,6},{9,7},{10,... | collective-permute-start | bytes 786440 | tf_op jit(solution)/shard_map/ppermute | solution.py:341
  32.1 5.1 %collective-permute-start.9 = (bf16[256,256]{1,0:T(8,128)(2,1)S(1)}, bf16[256,256]{1,0:T(8,128)(2,1)S(1)}, u32[]{:S(2)}, u32[]{:S(2)}) collective-permute-start(bf16[256,256]{1,0:T(8,128)(2,1)S(1)} %slice.24), channel_id=1, source_target_pairs={{0,2},{1,3},{2,4},{3,5},{4,6},{5,7},{6,8},{7,9},{8,10},{9,11},{10,... | collective-permute-start | bytes 393224 | tf_op jit(solution)/shard_map/ppermute | solution.py:341
  32.9 4.3 %collective-permute-start.10 = (bf16[256,256]{1,0:T(8,128)(2,1)S(1)}, bf16[256,256]{1,0:T(8,128)(2,1)S(1)}, u32[]{:S(2)}, u32[]{:S(2)}) collective-permute-start(bf16[256,256]{1,0:T(8,128)(2,1)S(1)} %slice.25), channel_id=1, source_target_pairs={{0,14},{1,15},{2,0},{3,1},{4,2},{5,3},{6,4},{7,5},{8,6},{9,7},{10,... | collective-permute-start | bytes 393224 | tf_op jit(solution)/shard_map/ppermute | solution.py:341
  38.1 5.3 %collective-permute-start.11 = (bf16[256,256]{1,0:T(8,128)(2,1)S(1)}, bf16[256,256]{1,0:T(8,128)(2,1)S(1)}, u32[]{:S(2)}, u32[]{:S(2)}) collective-permute-start(bf16[256,256]{1,0:T(8,128)(2,1)S(1)} %get-tuple-element.89), channel_id=1, source_target_pairs={{0,2},{1,3},{2,4},{3,5},{4,6},{5,7},{6,8},{7,9},{8,10},{9,11},{10,... | collective-permute-start | bytes 393224 | tf_op jit(solution)/shard_map/ppermute | solution.py:341
  39.3 6.4 %collective-permute-start.12 = (bf16[256,256]{1,0:T(8,128)(2,1)S(1)}, bf16[256,256]{1,0:T(8,128)(2,1)S(1)}, u32[]{:S(2)}, u32[]{:S(2)}) collective-permute-start(bf16[256,256]{1,0:T(8,128)(2,1)S(1)} %get-tuple-element.90), channel_id=1, source_target_pairs={{0,14},{1,15},{2,0},{3,1},{4,2},{5,3},{6,4},{7,5},{8,6},{9,7},{10,... | collective-permute-start | bytes 393224 | tf_op jit(solution)/shard_map/ppermute | solution.py:341
  45.9 6.5 %collective-permute-start.13 = (bf16[256,512]{1,0:T(8,128)(2,1)S(1)}, bf16[256,512]{1,0:T(8,128)(2,1)S(1)}, u32[]{:S(2)}, u32[]{:S(2)}) collective-permute-start(bf16[256,512]{1,0:T(8,128)(2,1)S(1)} %pad_maximum_fusion), channel_id=1, source_target_pairs={{0,2},{1,3},{2,4},{3,5},{4,6},{5,7},{6,8},{7,9},{8,10},{9,11},{10,... | collective-permute-start | bytes 786440 | tf_op jit(solution)/shard_map/ppermute | solution.py:341
  47.8 6.8 %collective-permute-start.14 = (bf16[256,512]{1,0:T(8,128)(2,1)S(1)}, bf16[256,512]{1,0:T(8,128)(2,1)S(1)}, u32[]{:S(2)}, u32[]{:S(2)}) collective-permute-start(bf16[256,512]{1,0:T(8,128)(2,1)S(1)} %pad_maximum_fusion.1), channel_id=1, source_target_pairs={{0,14},{1,15},{2,0},{3,1},{4,2},{5,3},{6,4},{7,5},{8,6},{9,7},{10,... | collective-permute-start | bytes 786440 | tf_op jit(solution)/shard_map/ppermute | solution.py:341
  54.7 6.9 %collective-permute-start.15 = (bf16[256,512]{1,0:T(8,128)(2,1)S(1)}, bf16[256,512]{1,0:T(8,128)(2,1)S(1)}, u32[]{:S(2)}, u32[]{:S(2)}) collective-permute-start(bf16[256,512]{1,0:T(8,128)(2,1)S(1)} %add_convert_fusion.4), channel_id=1, source_target_pairs={{0,2},{1,3},{2,4},{3,5},{4,6},{5,7},{6,8},{7,9},{8,10},{9,11},{10,... | collective-permute-start | bytes 786440 | tf_op jit(solution)/shard_map/ppermute | solution.py:341
  56.3 6.9 %collective-permute-start.16 = (bf16[256,512]{1,0:T(8,128)(2,1)S(1)}, bf16[256,512]{1,0:T(8,128)(2,1)S(1)}, u32[]{:S(2)}, u32[]{:S(2)}) collective-permute-start(bf16[256,512]{1,0:T(8,128)(2,1)S(1)} %add_convert_fusion.3), channel_id=1, source_target_pairs={{0,14},{1,15},{2,0},{3,1},{4,2},{5,3},{6,4},{7,5},{8,6},{9,7},{10,... | collective-permute-start | bytes 786440 | tf_op jit(solution)/shard_map/ppermute | solution.py:341
  63.3 17.6 %collective-permute-start.17 = (bf16[256,512]{1,0:T(8,128)(2,1)S(1)}, bf16[256,512]{1,0:T(8,128)(2,1)S(1)}, u32[]{:S(2)}, u32[]{:S(2)}) collective-permute-start(bf16[256,512]{1,0:T(8,128)(2,1)S(1)} %add_convert_fusion.2), channel_id=1, source_target_pairs={{0,2},{1,3},{2,4},{3,5},{4,6},{5,7},{6,8},{7,9},{8,10},{9,11},{10,... | collective-permute-start | bytes 786440 | tf_op jit(solution)/shard_map/ppermute | solution.py:341
  65.2 15.8 %collective-permute-start.18 = (bf16[256,512]{1,0:T(8,128)(2,1)S(1)}, bf16[256,512]{1,0:T(8,128)(2,1)S(1)}, u32[]{:S(2)}, u32[]{:S(2)}) collective-permute-start(bf16[256,512]{1,0:T(8,128)(2,1)S(1)} %add_convert_fusion.1), channel_id=1, source_target_pairs={{0,14},{1,15},{2,0},{3,1},{4,2},{5,3},{6,4},{7,5},{8,6},{9,7},{10,... | collective-permute-start | bytes 786440 | tf_op jit(solution)/shard_map/ppermute | solution.py:341
  69.6 12.9 %collective-permute-start.19 = (bf16[128,2048]{1,0:T(8,128)(2,1)S(1)}, bf16[128,2048]{1,0:T(8,128)(2,1)S(1)}, u32[]{:S(2)}, u32[]{:S(2)}) collective-permute-start(bf16[128,2048]{1,0:T(8,128)(2,1)S(1)} %get-tuple-element.125), channel_id=1, source_target_pairs={{0,1},{1,0},{2,3},{3,2},{4,5},{5,4},{6,7},{7,6},{8,9},{9,8},{10,11... | collective-permute-start | bytes 1572872 | tf_op jit(solution)/shard_map/ppermute | solution.py:336
  81.1 2.6 %collective-permute-start.20 = (bf16[128,512]{1,0:T(8,128)(2,1)S(1)}, bf16[128,512]{1,0:T(8,128)(2,1)S(1)}, u32[]{:S(2)}, u32[]{:S(2)}) collective-permute-start(bf16[128,512]{1,0:T(8,128)(2,1)S(1)} %pad_maximum_fusion.4), channel_id=1, source_target_pairs={{0,1},{1,0},{2,3},{3,2},{4,5},{5,4},{6,7},{7,6},{8,9},{9,8},{10,11... | collective-permute-start | bytes 393224 | tf_op jit(solution)/shard_map/ppermute | solution.py:336
where the time goes:
time: 85.4 us; the launch traced here: 85.1 us
  starting transfers between devices  38.6 us (45%)
  waiting for transfers between devices  23.5 us (28%)
  Pallas kernels  19.2 us (22%)
  other arithmetic  1.8 us (2%)
  between operations  1.06 us (1%)
  local copies, waits for them, and re-layouts  1.03 us (1%)
    ppermute x16, starting transfers between devices, ring(): return lax.ppermute(x, 'ctx', pairs)  25.1 us
    ppermute x16, waiting for transfers between devices, ring(): return lax.ppermute(x, 'ctx', pairs)  22 us
    pallas_call x11, Pallas kernels, call(): pl.pallas_call(kernel, out_shape=tuple(out), in_specs=in_specs, out_specs...  19.2 us
    ppermute x5, starting transfers between devices, swap(): return lax.ppermute(x, 'ctx', SWAP)  13.4 us
  transfers between devices with their start and end apart: 21, of which 12 were waited for; matrix products, arithmetic and copies ran while one was open for 2% of the time, Pallas kernels for 20%

commit v1 on v0

--- a/solution.py
+++ b/solution.py
@@ -275,8 +275,12 @@
     down_out[:, cols] = (td[:, cols].astype(F32) + down[...].astype(F32)).astype(BF16)
 
 
-def last_kernel(place, total, back, key, value, sem):
+def last_kernel(place, t0, up, down, back, key, value, total, sem):
     core = place[0]
+    for row in (0, 128):
+        rows = slice(row, row + 64)
+        part = t0[rows, :].astype(F32) + up[rows, :].astype(F32) + down[rows, :].astype(F32)
+        total[rows, :] = part.astype(BF16)
     mine, other = aligned(core, 256), aligned(1 - core, 256)
     copies = []
     for out, low in ((key, 0), (value, 256)):
@@ -425,14 +429,16 @@
         [pltpu.VMEM(DQT.shape, F32), acc], cost=5,
     )
     dq_got = swap(dq_par)
-    total = (t0.astype(F32) + up.astype(F32) + down.astype(F32)).astype(BF16)
-    away = jnp.concatenate([total[64:128], total[192:]], axis=0)
+    away = jnp.concatenate(
+        [sum(x[row:row + 64].astype(F32) for x in (t0, up, down)).astype(BF16) for row in (64, 192)],
+        axis=0,
+    )
     away, dq_own = together((away, dq_own))
     back = swap(away)
-    query_grad, total = together((join(dq_own, dq_got, core), total))
+    query_grad, up = together((join(dq_own, dq_got, core), up))
     key_grad, value_grad = call(
-        last_kernel, [shape((BLK, 512))] * 2, [place, total, back],
-        [pltpu.SemaphoreType.DMA((6,))], far_out=True,
+        last_kernel, [shape((BLK, 512))] * 2, [place, t0, up, down, back],
+        [pltpu.VMEM(TERM.shape, BF16), pltpu.SemaphoreType.DMA((6,))], far_out=True,
     )
     return (query_grad, key_grad, value_grad)
 

time: 85.4 us -> 85.9 us (level); the launches traced: 85.1 us -> 84.2 us
  waiting for transfers between devices: 23.5 us -> 13.8 us
  Pallas kernels: 19.2 us -> 28.6 us
    ppermute x16, waiting for transfers between devices: 22 us -> 12.2 us  [ring(): return lax.ppermute(x, 'ctx', pairs)]
    pallas_call x11, Pallas kernels: 19.2 us -> 28.6 us  [call(): pl.pallas_call(kernel, out_shape=tuple(out), in_specs=in_specs, out_specs...]
  transfers between devices with their start and end apart: 21 -> 21, of which waited for: 12 -> 9; matrix products, arithmetic and copies ran while one was open for 2% -> 2% of each run, Pallas kernels for 20% -> 30%
where the time goes in v1:
time: 85.9 us; the launch traced here: 84.2 us
  starting transfers between devices  37.9 us (44%)
  Pallas kernels  28.6 us (33%)
  waiting for transfers between devices  13.8 us (16%)
  other arithmetic  1.76 us (2%)
  between operations  1.08 us (1%)
  local copies, waits for them, and re-layouts  1.02 us (1%)
    pallas_call x11, Pallas kernels, call(): pl.pallas_call(kernel, out_shape=tuple(out), in_specs=in_specs, out_specs...  28.6 us
    ppermute x16, starting transfers between devices, ring(): return lax.ppermute(x, 'ctx', pairs)  25 us
    ppermute x5, starting transfers between devices, swap(): return lax.ppermute(x, 'ctx', SWAP)  12.9 us
    ppermute x16, waiting for transfers between devices, ring(): return lax.ppermute(x, 'ctx', pairs)  12.2 us
  transfers between devices with their start and end apart: 21, of which 9 were waited for; matrix products, arithmetic and copies ran while one was open for 2% of the time, Pallas kernels for 30%

profile of v1, /device:TPU:23, one launch (start us, length us, event | category | flops | bytes accessed | tf_op | source)
XLA Modules:
  0.0 84.2 jit_solution(16684028339888824450)
XLA Ops:
  4.6 1.7 %collective-permute-start.3 = (bf16[256,512]{1,0:T(8,128)(2,1)S(1)}, bf16[256,512]{1,0:T(8,128)(2,1)S(1)}, u32[]{:S(2)}, u32[]{:S(2)}) collective-permute-start(bf16[256,512]{1,0:T(8,128)(2,1)S(1)} %get-tuple-element.74), channel_id=1, source_target_pairs={{0,2},{1,3},{2,4},{3,5},{4,6},{5,7},{6,8},{7,9},{8,10},{9,11},{10,... | collective-permute-start | bytes 786440 | tf_op jit(solution)/shard_map/ppermute | solution.py:345
  6.3 4.0 %collective-permute-start.4 = (bf16[256,512]{1,0:T(8,128)(2,1)S(1)}, bf16[256,512]{1,0:T(8,128)(2,1)S(1)}, u32[]{:S(2)}, u32[]{:S(2)}) collective-permute-start(bf16[256,512]{1,0:T(8,128)(2,1)S(1)} %get-tuple-element.75), channel_id=1, source_target_pairs={{0,14},{1,15},{2,0},{3,1},{4,2},{5,3},{6,4},{7,5},{8,6},{9,7},{10,... | collective-permute-start | bytes 786440 | tf_op jit(solution)/shard_map/ppermute | solution.py:345
  10.4 3.6 %shard_map.77 = (s32[8]{0:T(128)S(1)}, s32[2,8,128]{2,1,0:T(8,128)S(1)}, bf16[4,1024,128]{2,1,0:T(8,128)(2,1)S(1)}, bf16[4,1024,128]{2,1,0:T(8,128)(2,1)S(1)}, f32[4,8,1024]{2,1,0:T(8,128)S(1)}) custom-call(s32[2]{0:T(128)S(1)} %pad_add_fusion.place, s32[16,128]{1,0:T(8,128)S(1)} %bitcast.3, bf16[128,4096]{1,0:T(8,128)(2,1)S(1)} %copy-done, ...), custom_call_target="tpu_custom_call" | custom-call | flops 3000000000 | bytes 1000000 | tf_op jit(solution)/shard_map/pallas_call | solution.py:325
  14.0 2.7 %collective-permute-done.3.up = bf16[256,512]{1,0:T(8,128)(2,1)S(1)} collective-permute-done((bf16[256,512]{1,0:T(8,128)(2,1)S(1)}, bf16[256,512]{1,0:T(8,128)(2,1)S(1)}, u32[]{:S(2)}, u32[]{:S(2)}) %collective-permute-start.3) | collective-permute-done | bytes 262176 | tf_op jit(solution)/shard_map/ppermute | solution.py:345
  16.7 2.7 %collective-permute-start.6 = (bf16[256,512]{1,0:T(8,128)(2,1)S(1)}, bf16[256,512]{1,0:T(8,128)(2,1)S(1)}, u32[]{:S(2)}, u32[]{:S(2)}) collective-permute-start(bf16[256,512]{1,0:T(8,128)(2,1)S(1)} %collective-permute-done.4.down), channel_id=1, source_target_pairs={{0,14},{1,15},{2,0},{3,1},{4,2},{5,3},{6,4},{7,5},{8,6},{9,7},{10,... | collective-permute-start | bytes 786440 | tf_op jit(solution)/shard_map/ppermute | solution.py:345
  19.3 2.2 %shard_map.78.state_in = f32[4,8,1024]{2,1,0:T(8,128)S(1)} custom-call(s32[8]{0:T(128)S(1)} %get-tuple-element.70.info, s32[2,8,128]{2,1,0:T(8,128)S(1)} %get-tuple-element.71.qrow, bf16[4,1024,128]{2,1,0:T(8,128)(2,1)S(1)} %get-tuple-element.72.qst, bf16[4,1024,128]{2,1,0:T(8,128)(2,1)S(1)} %get-tuple-element.73.dst, ...), custom_call_target="tpu_custom_call" | custom-call | flops 3000000000 | bytes 1000000 | tf_op jit(solution)/shard_map/pallas_call | solution.py:325
  21.6 3.3 %collective-permute-done.5.up = bf16[256,512]{1,0:T(8,128)(2,1)S(1)} collective-permute-done((bf16[256,512]{1,0:T(8,128)(2,1)S(1)}, bf16[256,512]{1,0:T(8,128)(2,1)S(1)}, u32[]{:S(2)}, u32[]{:S(2)}) %collective-permute-start.5) | collective-permute-done | bytes 262176 | tf_op jit(solution)/shard_map/ppermute | solution.py:345
  25.7 1.8 %collective-permute-start.8 = (bf16[256,512]{1,0:T(8,128)(2,1)S(1)}, bf16[256,512]{1,0:T(8,128)(2,1)S(1)}, u32[]{:S(2)}, u32[]{:S(2)}) collective-permute-start(bf16[256,512]{1,0:T(8,128)(2,1)S(1)} %collective-permute-done.6.down), channel_id=1, source_target_pairs={{0,14},{1,15},{2,0},{3,1},{4,2},{5,3},{6,4},{7,5},{8,6},{9,7},{10,... | collective-permute-start | bytes 786440 | tf_op jit(solution)/shard_map/ppermute | solution.py:345
  27.5 2.2 %shard_map.79.state_in = f32[4,8,1024]{2,1,0:T(8,128)S(1)} custom-call(s32[8]{0:T(128)S(1)} %get-tuple-element.70.info, s32[2,8,128]{2,1,0:T(8,128)S(1)} %get-tuple-element.71.qrow, bf16[4,1024,128]{2,1,0:T(8,128)(2,1)S(1)} %get-tuple-element.72.qst, bf16[4,1024,128]{2,1,0:T(8,128)(2,1)S(1)} %get-tuple-element.73.dst, ...), custom_call_target="tpu_custom_call" | custom-call | flops 3000000000 | bytes 1000000 | tf_op jit(solution)/shard_map/pallas_call | solution.py:325
  29.7 2.3 %collective-permute-done.7.up = bf16[256,512]{1,0:T(8,128)(2,1)S(1)} collective-permute-done((bf16[256,512]{1,0:T(8,128)(2,1)S(1)}, bf16[256,512]{1,0:T(8,128)(2,1)S(1)}, u32[]{:S(2)}, u32[]{:S(2)}) %collective-permute-start.7) | collective-permute-done | bytes 262176 | tf_op jit(solution)/shard_map/ppermute | solution.py:345
  32.9 1.9 %collective-permute-start.10 = (bf16[256,256]{1,0:T(8,128)(2,1)S(1)}, bf16[256,256]{1,0:T(8,128)(2,1)S(1)}, u32[]{:S(2)}, u32[]{:S(2)}) collective-permute-start(bf16[256,256]{1,0:T(8,128)(2,1)S(1)} %slice.37), channel_id=1, source_target_pairs={{0,14},{1,15},{2,0},{3,1},{4,2},{5,3},{6,4},{7,5},{8,6},{9,7},{10,... | collective-permute-start | bytes 393224 | tf_op jit(solution)/shard_map/ppermute | solution.py:345
  34.9 2.2 %shard_map.80.state_in = f32[4,8,1024]{2,1,0:T(8,128)S(1)} custom-call(s32[8]{0:T(128)S(1)} %get-tuple-element.70.info, s32[2,8,128]{2,1,0:T(8,128)S(1)} %get-tuple-element.71.qrow, bf16[4,1024,128]{2,1,0:T(8,128)(2,1)S(1)} %get-tuple-element.72.qst, bf16[4,1024,128]{2,1,0:T(8,128)(2,1)S(1)} %get-tuple-element.73.dst, ...), custom_call_target="tpu_custom_call" | custom-call | flops 3000000000 | bytes 1000000 | tf_op jit(solution)/shard_map/pallas_call | solution.py:325
  37.2 2.2 %shard_map.81 = (f32[4,8,1024]{2,1,0:T(8,128)S(1)}, bf16[256,256]{1,0:T(8,128)(2,1)S(1)}, bf16[256,256]{1,0:T(8,128)(2,1)S(1)}, bf16[6,128,1024]{2,1,0:T(8,128)(2,1)S(1)}) custom-call(s32[8]{0:T(128)S(1)} %get-tuple-element.70.info, s32[2,8,128]{2,1,0:T(8,128)S(1)} %get-tuple-element.71.qrow, bf16[4,1024,128]{2,1,0:T(8,128)(2,1)S(1)} %get-tuple-element.72.qst, ...), custom_call_target="tpu_custom_call" | custom-call | flops 3000000000 | bytes 1000000 | tf_op jit(solution)/shard_map/pallas_call | solution.py:325
  40.7 1.7 %collective-permute-start.12 = (bf16[256,256]{1,0:T(8,128)(2,1)S(1)}, bf16[256,256]{1,0:T(8,128)(2,1)S(1)}, u32[]{:S(2)}, u32[]{:S(2)}) collective-permute-start(bf16[256,256]{1,0:T(8,128)(2,1)S(1)} %get-tuple-element.90), channel_id=1, source_target_pairs={{0,14},{1,15},{2,0},{3,1},{4,2},{5,3},{6,4},{7,5},{8,6},{9,7},{10,... | collective-permute-start | bytes 393224 | tf_op jit(solution)/shard_map/ppermute | solution.py:345
  42.4 3.4 %shard_map.82 = (bf16[256,512]{1,0:T(8,128)(2,1)S(1)}, bf16[256,512]{1,0:T(8,128)(2,1)S(1)}, f32[4,128,1024]{2,1,0:T(8,128)S(1)}) custom-call(s32[8]{0:T(128)S(1)} %get-tuple-element.70.info, s32[2,8,128]{2,1,0:T(8,128)S(1)} %get-tuple-element.71.qrow, bf16[4,1024,128]{2,1,0:T(8,128)(2,1)S(1)} %get-tuple-element.72.qst, ...), custom_call_target="tpu_custom_call" | custom-call | flops 5000000000 | bytes 1000000 | tf_op jit(solution)/shard_map/pallas_call | solution.py:325
  46.2 2.6 %collective-permute-start.14 = (bf16[256,512]{1,0:T(8,128)(2,1)S(1)}, bf16[256,512]{1,0:T(8,128)(2,1)S(1)}, u32[]{:S(2)}, u32[]{:S(2)}) collective-permute-start(bf16[256,512]{1,0:T(8,128)(2,1)S(1)} %pad_maximum_fusion.1), channel_id=1, source_target_pairs={{0,14},{1,15},{2,0},{3,1},{4,2},{5,3},{6,4},{7,5},{8,6},{9,7},{10,... | collective-permute-start | bytes 786440 | tf_op jit(solution)/shard_map/ppermute | solution.py:345
  48.7 4.0 %shard_map.83 = (bf16[256,512]{1,0:T(8,128)(2,1)S(1)}, bf16[256,512]{1,0:T(8,128)(2,1)S(1)}, f32[4,128,1024]{2,1,0:T(8,128)S(1)}) custom-call(s32[8]{0:T(128)S(1)} %get-tuple-element.70.info, s32[2,8,128]{2,1,0:T(8,128)S(1)} %get-tuple-element.71.qrow, bf16[4,1024,128]{2,1,0:T(8,128)(2,1)S(1)} %get-tuple-element.72.qst, ...), custom_call_target="tpu_custom_call" | custom-call | flops 5000000000 | bytes 1000000 | tf_op jit(solution)/shard_map/pallas_call | solution.py:325
  52.9 1.5 %collective-permute-start.15 = (bf16[256,512]{1,0:T(8,128)(2,1)S(1)}, bf16[256,512]{1,0:T(8,128)(2,1)S(1)}, u32[]{:S(2)}, u32[]{:S(2)}) collective-permute-start(bf16[256,512]{1,0:T(8,128)(2,1)S(1)} %add_convert_fusion.3), channel_id=1, source_target_pairs={{0,2},{1,3},{2,4},{3,5},{4,6},{5,7},{6,8},{7,9},{8,10},{9,11},{10,... | collective-permute-start | bytes 786440 | tf_op jit(solution)/shard_map/ppermute | solution.py:345
  55.7 3.4 %shard_map.84 = (bf16[256,512]{1,0:T(8,128)(2,1)S(1)}, bf16[256,512]{1,0:T(8,128)(2,1)S(1)}, f32[4,128,1024]{2,1,0:T(8,128)S(1)}) custom-call(s32[8]{0:T(128)S(1)} %get-tuple-element.70.info, s32[2,8,128]{2,1,0:T(8,128)S(1)} %get-tuple-element.71.qrow, bf16[4,1024,128]{2,1,0:T(8,128)(2,1)S(1)} %get-tuple-element.72.qst, ...), custom_call_target="tpu_custom_call" | custom-call | flops 5000000000 | bytes 1000000 | tf_op jit(solution)/shard_map/pallas_call | solution.py:325
  59.1 3.4 %collective-permute-done.15 = bf16[256,512]{1,0:T(8,128)(2,1)S(1)} collective-permute-done((bf16[256,512]{1,0:T(8,128)(2,1)S(1)}, bf16[256,512]{1,0:T(8,128)(2,1)S(1)}, u32[]{:S(2)}, u32[]{:S(2)}) %collective-permute-start.15) | collective-permute-done | bytes 262176 | tf_op jit(solution)/shard_map/ppermute | solution.py:345
  63.9 1.7 %collective-permute-start.18 = (bf16[256,512]{1,0:T(8,128)(2,1)S(1)}, bf16[256,512]{1,0:T(8,128)(2,1)S(1)}, u32[]{:S(2)}, u32[]{:S(2)}) collective-permute-start(bf16[256,512]{1,0:T(8,128)(2,1)S(1)} %add_convert_fusion), channel_id=1, source_target_pairs={{0,14},{1,15},{2,0},{3,1},{4,2},{5,3},{6,4},{7,5},{8,6},{9,7},{10,... | collective-permute-start | bytes 786440 | tf_op jit(solution)/shard_map/ppermute | solution.py:345
  65.6 3.5 %shard_map.85 = (bf16[256,512]{1,0:T(8,128)(2,1)S(1)}, bf16[128,2048]{1,0:T(8,128)(2,1)S(1)}, bf16[128,2048]{1,0:T(8,128)(2,1)S(1)}) custom-call(s32[8]{0:T(128)S(1)} %get-tuple-element.70.info, s32[2,8,128]{2,1,0:T(8,128)S(1)} %get-tuple-element.71.qrow, bf16[4,1024,128]{2,1,0:T(8,128)(2,1)S(1)} %get-tuple-element.72.qst, ...), custom_call_target="tpu_custom_call" | custom-call | flops 5000000000 | bytes 1000000 | tf_op jit(solution)/shard_map/pallas_call | solution.py:325
  69.2 10.8 %collective-permute-start.19 = (bf16[128,2048]{1,0:T(8,128)(2,1)S(1)}, bf16[128,2048]{1,0:T(8,128)(2,1)S(1)}, u32[]{:S(2)}, u32[]{:S(2)}) collective-permute-start(bf16[128,2048]{1,0:T(8,128)(2,1)S(1)} %get-tuple-element.125), channel_id=1, source_target_pairs={{0,1},{1,0},{2,3},{3,2},{4,5},{5,4},{6,7},{7,6},{8,9},{9,8},{10,11... | collective-permute-start | bytes 1572872 | tf_op jit(solution)/shard_map/ppermute | solution.py:340
  82.7 1.3 %shard_map.86 = (bf16[128,512]{1,0:T(8,128)(2,1)}, bf16[128,512]{1,0:T(8,128)(2,1)}) custom-call(s32[2]{0:T(128)S(1)} %pad_add_fusion.place, bf16[256,512]{1,0:T(8,128)(2,1)S(1)} %get-tuple-element.116.t0, bf16[256,512]{1,0:T(8,128)(2,1)S(1)} %collective-permute-done.17.up, bf16[256,512]{1,0:T(8,128)(2,1)S(1)} %collective-permute-done.18.down, ...), custom_call_target="tpu_custom_call" | custom-call | flops 3000000000 | bytes 1000000 | tf_op jit(solution)/shard_map/pallas_call | solution.py:325
  (54 shorter events, 13.0 us)
Async XLA Ops:
  1.6 1.7 %collective-permute-start = (bf16[128,512]{1,0:T(8,128)(2,1)S(1)}, bf16[128,512]{1,0:T(8,128)(2,1)S(1)}, u32[]{:S(2)}, u32[]{:S(2)}) collective-permute-start(bf16[128,512]{1,0:T(8,128)(2,1)S(1)} %pad_maximum_fusion.2), channel_id=1, source_target_pairs={{0,1},{1,0},{2,3},{3,2},{4,5},{5,4},{6,7},{7,6},{8,9},{9,8},{10,11... | collective-permute-start | bytes 393224 | tf_op jit(solution)/shard_map/ppermute | solution.py:340
  3.4 7.0 %collective-permute-start.1 = (bf16[128,4096]{1,0:T(8,128)(2,1)}, bf16[128,4096]{1,0:T(8,128)(2,1)S(1)}, u32[]{:S(2)}, u32[]{:S(2)}) collective-permute-start(bf16[128,4096]{1,0:T(8,128)(2,1)} %q_own.1), channel_id=1, source_target_pairs={{0,1},{1,0},{2,3},{3,2},{4,5},{5,4},{6,7},{7,6},{8,9},{9,8},{10,11... | collective-permute-start | bytes 3145736 | tf_op jit(solution)/shard_map/ppermute | solution.py:340
  3.7 6.6 %collective-permute-start.2 = (bf16[128,4096]{1,0:T(8,128)(2,1)}, bf16[128,4096]{1,0:T(8,128)(2,1)S(1)}, u32[]{:S(2)}, u32[]{:S(2)}) collective-permute-start(bf16[128,4096]{1,0:T(8,128)(2,1)} %do_own.1), channel_id=1, source_target_pairs={{0,1},{1,0},{2,3},{3,2},{4,5},{5,4},{6,7},{7,6},{8,9},{9,8},{10,11... | collective-permute-start | bytes 3145736 | tf_op jit(solution)/shard_map/ppermute | solution.py:340
  4.0 6.4 %copy-start = (bf16[128,4096]{1,0:T(8,128)(2,1)S(1)}, bf16[128,4096]{1,0:T(8,128)(2,1)}, u32[]{:S(2)}) copy-start(bf16[128,4096]{1,0:T(8,128)(2,1)} %q_own.1) | copy-start | bytes 3145732
  4.0 6.4 %copy-start.1 = (bf16[128,4096]{1,0:T(8,128)(2,1)S(1)}, bf16[128,4096]{1,0:T(8,128)(2,1)}, u32[]{:S(2)}) copy-start(bf16[128,4096]{1,0:T(8,128)(2,1)} %do_own.1) | copy-start | bytes 3145732
  4.0 6.4 %copy-start.2 = (s32[2048]{0:T(1024)S(1)}, s32[2048]{0:T(1024)}, u32[]{:S(2)}) copy-start(s32[2048]{0:T(1024)} %param.9) | copy-start | bytes 24580
  4.6 12.0 %collective-permute-start.3 = (bf16[256,512]{1,0:T(8,128)(2,1)S(1)}, bf16[256,512]{1,0:T(8,128)(2,1)S(1)}, u32[]{:S(2)}, u32[]{:S(2)}) collective-permute-start(bf16[256,512]{1,0:T(8,128)(2,1)S(1)} %get-tuple-element.74), channel_id=1, source_target_pairs={{0,2},{1,3},{2,4},{3,5},{4,6},{5,7},{6,8},{7,9},{8,10},{9,11},{10,... | collective-permute-start | bytes 786440 | tf_op jit(solution)/shard_map/ppermute | solution.py:345
  6.3 10.3 %collective-permute-start.4 = (bf16[256,512]{1,0:T(8,128)(2,1)S(1)}, bf16[256,512]{1,0:T(8,128)(2,1)S(1)}, u32[]{:S(2)}, u32[]{:S(2)}) collective-permute-start(bf16[256,512]{1,0:T(8,128)(2,1)S(1)} %get-tuple-element.75), channel_id=1, source_target_pairs={{0,14},{1,15},{2,0},{3,1},{4,2},{5,3},{6,4},{7,5},{8,6},{9,7},{10,... | collective-permute-start | bytes 786440 | tf_op jit(solution)/shard_map/ppermute | solution.py:345
  16.7 8.2 %collective-permute-start.5 = (bf16[256,512]{1,0:T(8,128)(2,1)S(1)}, bf16[256,512]{1,0:T(8,128)(2,1)S(1)}, u32[]{:S(2)}, u32[]{:S(2)}) collective-permute-start(bf16[256,512]{1,0:T(8,128)(2,1)S(1)} %collective-permute-done.3.up), channel_id=1, source_target_pairs={{0,2},{1,3},{2,4},{3,5},{4,6},{5,7},{6,8},{7,9},{8,10},{9,11},{10,... | collective-permute-start | bytes 786440 | tf_op jit(solution)/shard_map/ppermute | solution.py:345
  16.7 8.2 %collective-permute-start.6 = (bf16[256,512]{1,0:T(8,128)(2,1)S(1)}, bf16[256,512]{1,0:T(8,128)(2,1)S(1)}, u32[]{:S(2)}, u32[]{:S(2)}) collective-permute-start(bf16[256,512]{1,0:T(8,128)(2,1)S(1)} %collective-permute-done.4.down), channel_id=1, source_target_pairs={{0,14},{1,15},{2,0},{3,1},{4,2},{5,3},{6,4},{7,5},{8,6},{9,7},{10,... | collective-permute-start | bytes 786440 | tf_op jit(solution)/shard_map/ppermute | solution.py:345
  24.8 7.2 %collective-permute-start.7 = (bf16[256,512]{1,0:T(8,128)(2,1)S(1)}, bf16[256,512]{1,0:T(8,128)(2,1)S(1)}, u32[]{:S(2)}, u32[]{:S(2)}) collective-permute-start(bf16[256,512]{1,0:T(8,128)(2,1)S(1)} %collective-permute-done.5.up), channel_id=1, source_target_pairs={{0,2},{1,3},{2,4},{3,5},{4,6},{5,7},{6,8},{7,9},{8,10},{9,11},{10,... | collective-permute-start | bytes 786440 | tf_op jit(solution)/shard_map/ppermute | solution.py:345
  25.7 6.4 %collective-permute-start.8 = (bf16[256,512]{1,0:T(8,128)(2,1)S(1)}, bf16[256,512]{1,0:T(8,128)(2,1)S(1)}, u32[]{:S(2)}, u32[]{:S(2)}) collective-permute-start(bf16[256,512]{1,0:T(8,128)(2,1)S(1)} %collective-permute-done.6.down), channel_id=1, source_target_pairs={{0,14},{1,15},{2,0},{3,1},{4,2},{5,3},{6,4},{7,5},{8,6},{9,7},{10,... | collective-permute-start | bytes 786440 | tf_op jit(solution)/shard_map/ppermute | solution.py:345
  32.1 5.1 %collective-permute-start.9 = (bf16[256,256]{1,0:T(8,128)(2,1)S(1)}, bf16[256,256]{1,0:T(8,128)(2,1)S(1)}, u32[]{:S(2)}, u32[]{:S(2)}) collective-permute-start(bf16[256,256]{1,0:T(8,128)(2,1)S(1)} %slice.36), channel_id=1, source_target_pairs={{0,2},{1,3},{2,4},{3,5},{4,6},{5,7},{6,8},{7,9},{8,10},{9,11},{10,... | collective-permute-start | bytes 393224 | tf_op jit(solution)/shard_map/ppermute | solution.py:345
  32.9 4.3 %collective-permute-start.10 = (bf16[256,256]{1,0:T(8,128)(2,1)S(1)}, bf16[256,256]{1,0:T(8,128)(2,1)S(1)}, u32[]{:S(2)}, u32[]{:S(2)}) collective-permute-start(bf16[256,256]{1,0:T(8,128)(2,1)S(1)} %slice.37), channel_id=1, source_target_pairs={{0,14},{1,15},{2,0},{3,1},{4,2},{5,3},{6,4},{7,5},{8,6},{9,7},{10,... | collective-permute-start | bytes 393224 | tf_op jit(solution)/shard_map/ppermute | solution.py:345
  39.4 6.3 %collective-permute-start.11 = (bf16[256,256]{1,0:T(8,128)(2,1)S(1)}, bf16[256,256]{1,0:T(8,128)(2,1)S(1)}, u32[]{:S(2)}, u32[]{:S(2)}) collective-permute-start(bf16[256,256]{1,0:T(8,128)(2,1)S(1)} %get-tuple-element.89), channel_id=1, source_target_pairs={{0,2},{1,3},{2,4},{3,5},{4,6},{5,7},{6,8},{7,9},{8,10},{9,11},{10,... | collective-permute-start | bytes 393224 | tf_op jit(solution)/shard_map/ppermute | solution.py:345
  40.7 5.1 %collective-permute-start.12 = (bf16[256,256]{1,0:T(8,128)(2,1)S(1)}, bf16[256,256]{1,0:T(8,128)(2,1)S(1)}, u32[]{:S(2)}, u32[]{:S(2)}) collective-permute-start(bf16[256,256]{1,0:T(8,128)(2,1)S(1)} %get-tuple-element.90), channel_id=1, source_target_pairs={{0,14},{1,15},{2,0},{3,1},{4,2},{5,3},{6,4},{7,5},{8,6},{9,7},{10,... | collective-permute-start | bytes 393224 | tf_op jit(solution)/shard_map/ppermute | solution.py:345
  46.0 6.7 %collective-permute-start.13 = (bf16[256,512]{1,0:T(8,128)(2,1)S(1)}, bf16[256,512]{1,0:T(8,128)(2,1)S(1)}, u32[]{:S(2)}, u32[]{:S(2)}) collective-permute-start(bf16[256,512]{1,0:T(8,128)(2,1)S(1)} %pad_maximum_fusion), channel_id=1, source_target_pairs={{0,2},{1,3},{2,4},{3,5},{4,6},{5,7},{6,8},{7,9},{8,10},{9,11},{10,... | collective-permute-start | bytes 786440 | tf_op jit(solution)/shard_map/ppermute | solution.py:345
  46.2 6.6 %collective-permute-start.14 = (bf16[256,512]{1,0:T(8,128)(2,1)S(1)}, bf16[256,512]{1,0:T(8,128)(2,1)S(1)}, u32[]{:S(2)}, u32[]{:S(2)}) collective-permute-start(bf16[256,512]{1,0:T(8,128)(2,1)S(1)} %pad_maximum_fusion.1), channel_id=1, source_target_pairs={{0,14},{1,15},{2,0},{3,1},{4,2},{5,3},{6,4},{7,5},{8,6},{9,7},{10,... | collective-permute-start | bytes 786440 | tf_op jit(solution)/shard_map/ppermute | solution.py:345
  52.9 9.6 %collective-permute-start.15 = (bf16[256,512]{1,0:T(8,128)(2,1)S(1)}, bf16[256,512]{1,0:T(8,128)(2,1)S(1)}, u32[]{:S(2)}, u32[]{:S(2)}) collective-permute-start(bf16[256,512]{1,0:T(8,128)(2,1)S(1)} %add_convert_fusion.3), channel_id=1, source_target_pairs={{0,2},{1,3},{2,4},{3,5},{4,6},{5,7},{6,8},{7,9},{8,10},{9,11},{10,... | collective-permute-start | bytes 786440 | tf_op jit(solution)/shard_map/ppermute | solution.py:345
  54.4 8.3 %collective-permute-start.16 = (bf16[256,512]{1,0:T(8,128)(2,1)S(1)}, bf16[256,512]{1,0:T(8,128)(2,1)S(1)}, u32[]{:S(2)}, u32[]{:S(2)}) collective-permute-start(bf16[256,512]{1,0:T(8,128)(2,1)S(1)} %add_convert_fusion.2), channel_id=1, source_target_pairs={{0,14},{1,15},{2,0},{3,1},{4,2},{5,3},{6,4},{7,5},{8,6},{9,7},{10,... | collective-permute-start | bytes 786440 | tf_op jit(solution)/shard_map/ppermute | solution.py:345
  62.9 17.1 %collective-permute-start.17 = (bf16[256,512]{1,0:T(8,128)(2,1)S(1)}, bf16[256,512]{1,0:T(8,128)(2,1)S(1)}, u32[]{:S(2)}, u32[]{:S(2)}) collective-permute-start(bf16[256,512]{1,0:T(8,128)(2,1)S(1)} %add_convert_fusion.1), channel_id=1, source_target_pairs={{0,2},{1,3},{2,4},{3,5},{4,6},{5,7},{6,8},{7,9},{8,10},{9,11},{10,... | collective-permute-start | bytes 786440 | tf_op jit(solution)/shard_map/ppermute | solution.py:345
  63.9 16.0 %collective-permute-start.18 = (bf16[256,512]{1,0:T(8,128)(2,1)S(1)}, bf16[256,512]{1,0:T(8,128)(2,1)S(1)}, u32[]{:S(2)}, u32[]{:S(2)}) collective-permute-start(bf16[256,512]{1,0:T(8,128)(2,1)S(1)} %add_convert_fusion), channel_id=1, source_target_pairs={{0,14},{1,15},{2,0},{3,1},{4,2},{5,3},{6,4},{7,5},{8,6},{9,7},{10,... | collective-permute-start | bytes 786440 | tf_op jit(solution)/shard_map/ppermute | solution.py:345
  69.2 12.3 %collective-permute-start.19 = (bf16[128,2048]{1,0:T(8,128)(2,1)S(1)}, bf16[128,2048]{1,0:T(8,128)(2,1)S(1)}, u32[]{:S(2)}, u32[]{:S(2)}) collective-permute-start(bf16[128,2048]{1,0:T(8,128)(2,1)S(1)} %get-tuple-element.125), channel_id=1, source_target_pairs={{0,1},{1,0},{2,3},{3,2},{4,5},{5,4},{6,7},{7,6},{8,9},{9,8},{10,11... | collective-permute-start | bytes 1572872 | tf_op jit(solution)/shard_map/ppermute | solution.py:340
  80.0 2.7 %collective-permute-start.20 = (bf16[128,512]{1,0:T(8,128)(2,1)S(1)}, bf16[128,512]{1,0:T(8,128)(2,1)S(1)}, u32[]{:S(2)}, u32[]{:S(2)}) collective-permute-start(bf16[128,512]{1,0:T(8,128)(2,1)S(1)} %pad_maximum_fusion.4), channel_id=1, source_target_pairs={{0,1},{1,0},{2,3},{3,2},{4,5},{5,4},{6,7},{7,6},{8,9},{9,8},{10,11... | collective-permute-start | bytes 393224 | tf_op jit(solution)/shard_map/ppermute | solution.py:340

commit v2 on v0

--- a/solution.py
+++ b/solution.py
@@ -336,6 +336,13 @@
     return lax.ppermute(x, "ctx", SWAP)
 
 
+def cross_ring(x, step):
+    pairs = [
+        (2 * z + c, 2 * ((z + step * (1 - 2 * c)) % NZ) + c) for z in range(NZ) for c in range(2)
+    ]
+    return lax.ppermute(x, "ctx", pairs)
+
+
 def ring(x, step):
     pairs = [(2 * z + c, 2 * ((z + step) % NZ) + c) for z in range(NZ) for c in range(2)]
     return lax.ppermute(x, "ctx", pairs)
@@ -371,7 +378,7 @@
     together = lax.optimization_barrier
     q_in, do_in, unused = together((queries, grad_output, got))
     q_par, do_par = swap(q_in), swap(do_in)
-    up, down = ring(own_up, 1), ring(own_down, -1)
+    up, down = cross_ring(own_up, 1), cross_ring(own_down, -1)
     info, qrow, qst, dst, state = call(
         open_kernel,
         [INFO, QROW, STACK, STACK, STATE],
@@ -383,6 +390,8 @@
     ups, downs = [], []
     for k in (1, 2, 3):
         up, down, state = together((up, down, state))
+        if k == 1:
+            up, down = together((jnp.where(core == 0, up, down), jnp.where(core == 0, down, up)))
         ups.append(up)
         downs.append(down)
         if k < 3:

time: 85.4 us -> 85.7 us (level); the launches traced: 85.1 us -> 84.1 us
  waiting for transfers between devices: 23.5 us -> 13.6 us
  Pallas kernels: 19.2 us -> 28.6 us
    ppermute x16 -> x14, waiting for transfers between devices: 22 us -> 8.58 us  [ring(): return lax.ppermute(x, 'ctx', pairs)]
    pallas_call x11, Pallas kernels: 19.2 us -> 28.6 us  [call(): pl.pallas_call(kernel, out_shape=tuple(out), in_specs=in_specs, out_specs...]
    ppermute x16 -> x14, starting transfers between devices: 25.1 us -> 19.3 us  [ring(): return lax.ppermute(x, 'ctx', pairs)]
    ppermute x0 -> x2, starting transfers between devices: none -> 5.65 us  [cross_ring(): return lax.ppermute(x, 'ctx', pairs)]
    ppermute x0 -> x2, waiting for transfers between devices: none -> 3.48 us  [cross_ring(): return lax.ppermute(x, 'ctx', pairs)]
  transfers between devices with their start and end apart: 21 -> 21, of which waited for: 12 -> 9; matrix products, arithmetic and copies ran while one was open for 2% -> 2% of each run, Pallas kernels for 20% -> 30%
where the time goes in v2:
time: 85.7 us; the launch traced here: 84.1 us
  starting transfers between devices  37.9 us (44%)
  Pallas kernels  28.6 us (33%)
  waiting for transfers between devices  13.6 us (16%)
  other arithmetic  1.84 us (2%)
  between operations  1.15 us (1%)
  local copies, waits for them, and re-layouts  1.03 us (1%)
    pallas_call x11, Pallas kernels, call(): pl.pallas_call(kernel, out_shape=tuple(out), in_specs=in_specs, out_specs...  28.6 us
    ppermute x14, starting transfers between devices, ring(): return lax.ppermute(x, 'ctx', pairs)  19.3 us
    ppermute x5, starting transfers between devices, swap(): return lax.ppermute(x, 'ctx', SWAP)  12.9 us
    ppermute x14, waiting for transfers between devices, ring(): return lax.ppermute(x, 'ctx', pairs)  8.58 us
    ppermute x2, starting transfers between devices, cross_ring(): return lax.ppermute(x, 'ctx', pairs)  5.65 us
    ppermute x2, waiting for transfers between devices, cross_ring(): return lax.ppermute(x, 'ctx', pairs)  3.48 us
  transfers between devices with their start and end apart: 21, of which 9 were waited for; matrix products, arithmetic and copies ran while one was open for 2% of the time, Pallas kernels for 30%

profile of v2, /device:TPU:23, one launch (start us, length us, event | category | flops | bytes accessed | tf_op | source)
XLA Modules:
  0.0 84.1 jit_solution(16611936017299335154)
XLA Ops:
  4.6 5.7 %collective-permute-start.3 = (bf16[256,512]{1,0:T(8,128)(2,1)S(1)}, bf16[256,512]{1,0:T(8,128)(2,1)S(1)}, u32[]{:S(2)}, u32[]{:S(2)}) collective-permute-start(bf16[256,512]{1,0:T(8,128)(2,1)S(1)} %get-tuple-element.76), channel_id=1, source_target_pairs={{0,2},{1,15},{2,4},{3,1},{4,6},{5,3},{6,8},{7,5},{8,10},{9,7},{10,... | collective-permute-start | bytes 786440 | tf_op jit(solution)/shard_map/ppermute | solution.py:343
  10.3 3.6 %shard_map.77 = (s32[8]{0:T(128)S(1)}, s32[2,8,128]{2,1,0:T(8,128)S(1)}, bf16[4,1024,128]{2,1,0:T(8,128)(2,1)S(1)}, bf16[4,1024,128]{2,1,0:T(8,128)(2,1)S(1)}, f32[4,8,1024]{2,1,0:T(8,128)S(1)}) custom-call(s32[2]{0:T(128)S(1)} %pad_add_fusion.place, s32[16,128]{1,0:T(8,128)S(1)} %bitcast.3, bf16[128,4096]{1,0:T(8,128)(2,1)S(1)} %copy-done, ...), custom_call_target="tpu_custom_call" | custom-call | flops 3000000000 | bytes 1000000 | tf_op jit(solution)/shard_map/pallas_call | solution.py:321
  13.9 1.6 %collective-permute-done.3 = bf16[256,512]{1,0:T(8,128)(2,1)S(1)} collective-permute-done((bf16[256,512]{1,0:T(8,128)(2,1)S(1)}, bf16[256,512]{1,0:T(8,128)(2,1)S(1)}, u32[]{:S(2)}, u32[]{:S(2)}) %collective-permute-start.3) | collective-permute-done | bytes 262176 | tf_op jit(solution)/shard_map/ppermute | solution.py:343
  15.5 1.9 %collective-permute-done.4 = bf16[256,512]{1,0:T(8,128)(2,1)S(1)} collective-permute-done((bf16[256,512]{1,0:T(8,128)(2,1)S(1)}, bf16[256,512]{1,0:T(8,128)(2,1)S(1)}, u32[]{:S(2)}, u32[]{:S(2)}) %collective-permute-start.4) | collective-permute-done | bytes 262176 | tf_op jit(solution)/shard_map/ppermute | solution.py:343
  17.5 2.7 %collective-permute-start.6 = (bf16[256,512]{1,0:T(8,128)(2,1)S(1)}, bf16[256,512]{1,0:T(8,128)(2,1)S(1)}, u32[]{:S(2)}, u32[]{:S(2)}) collective-permute-start(bf16[256,512]{1,0:T(8,128)(2,1)S(1)} %get-tuple-element.82.down), channel_id=1, source_target_pairs={{0,14},{1,15},{2,0},{3,1},{4,2},{5,3},{6,4},{7,5},{8,6},{9,7},{10,... | collective-permute-start | bytes 786440 | tf_op jit(solution)/shard_map/ppermute | solution.py:348
  20.2 2.2 %shard_map.78.state_in = f32[4,8,1024]{2,1,0:T(8,128)S(1)} custom-call(s32[8]{0:T(128)S(1)} %get-tuple-element.72.info, s32[2,8,128]{2,1,0:T(8,128)S(1)} %get-tuple-element.73.qrow, bf16[4,1024,128]{2,1,0:T(8,128)(2,1)S(1)} %get-tuple-element.74.qst, bf16[4,1024,128]{2,1,0:T(8,128)(2,1)S(1)} %get-tuple-element.75.dst, ...), custom_call_target="tpu_custom_call" | custom-call | flops 3000000000 | bytes 1000000 | tf_op jit(solution)/shard_map/pallas_call | solution.py:321
  22.4 4.3 %collective-permute-done.5.up = bf16[256,512]{1,0:T(8,128)(2,1)S(1)} collective-permute-done((bf16[256,512]{1,0:T(8,128)(2,1)S(1)}, bf16[256,512]{1,0:T(8,128)(2,1)S(1)}, u32[]{:S(2)}, u32[]{:S(2)}) %collective-permute-start.5) | collective-permute-done | bytes 262176 | tf_op jit(solution)/shard_map/ppermute | solution.py:348
  26.7 2.7 %collective-permute-start.8 = (bf16[256,512]{1,0:T(8,128)(2,1)S(1)}, bf16[256,512]{1,0:T(8,128)(2,1)S(1)}, u32[]{:S(2)}, u32[]{:S(2)}) collective-permute-start(bf16[256,512]{1,0:T(8,128)(2,1)S(1)} %collective-permute-done.6.down), channel_id=1, source_target_pairs={{0,14},{1,15},{2,0},{3,1},{4,2},{5,3},{6,4},{7,5},{8,6},{9,7},{10,... | collective-permute-start | bytes 786440 | tf_op jit(solution)/shard_map/ppermute | solution.py:348
  29.4 2.2 %shard_map.79.state_in = f32[4,8,1024]{2,1,0:T(8,128)S(1)} custom-call(s32[8]{0:T(128)S(1)} %get-tuple-element.72.info, s32[2,8,128]{2,1,0:T(8,128)S(1)} %get-tuple-element.73.qrow, bf16[4,1024,128]{2,1,0:T(8,128)(2,1)S(1)} %get-tuple-element.74.qst, bf16[4,1024,128]{2,1,0:T(8,128)(2,1)S(1)} %get-tuple-element.75.dst, ...), custom_call_target="tpu_custom_call" | custom-call | flops 3000000000 | bytes 1000000 | tf_op jit(solution)/shard_map/pallas_call | solution.py:321
  31.6 3.4 %collective-permute-done.7.up = bf16[256,512]{1,0:T(8,128)(2,1)S(1)} collective-permute-done((bf16[256,512]{1,0:T(8,128)(2,1)S(1)}, bf16[256,512]{1,0:T(8,128)(2,1)S(1)}, u32[]{:S(2)}, u32[]{:S(2)}) %collective-permute-start.7) | collective-permute-done | bytes 262176 | tf_op jit(solution)/shard_map/ppermute | solution.py:348
  35.2 2.7 %collective-permute-start.10 = (bf16[256,256]{1,0:T(8,128)(2,1)S(1)}, bf16[256,256]{1,0:T(8,128)(2,1)S(1)}, u32[]{:S(2)}, u32[]{:S(2)}) collective-permute-start(bf16[256,256]{1,0:T(8,128)(2,1)S(1)} %slice.25), channel_id=1, source_target_pairs={{0,14},{1,15},{2,0},{3,1},{4,2},{5,3},{6,4},{7,5},{8,6},{9,7},{10,... | collective-permute-start | bytes 393224 | tf_op jit(solution)/shard_map/ppermute | solution.py:348
  37.8 2.2 %shard_map.80.state_in = f32[4,8,1024]{2,1,0:T(8,128)S(1)} custom-call(s32[8]{0:T(128)S(1)} %get-tuple-element.72.info, s32[2,8,128]{2,1,0:T(8,128)S(1)} %get-tuple-element.73.qrow, bf16[4,1024,128]{2,1,0:T(8,128)(2,1)S(1)} %get-tuple-element.74.qst, bf16[4,1024,128]{2,1,0:T(8,128)(2,1)S(1)} %get-tuple-element.75.dst, ...), custom_call_target="tpu_custom_call" | custom-call | flops 3000000000 | bytes 1000000 | tf_op jit(solution)/shard_map/pallas_call | solution.py:321
  40.2 2.2 %shard_map.81 = (f32[4,8,1024]{2,1,0:T(8,128)S(1)}, bf16[256,256]{1,0:T(8,128)(2,1)S(1)}, bf16[256,256]{1,0:T(8,128)(2,1)S(1)}, bf16[6,128,1024]{2,1,0:T(8,128)(2,1)S(1)}) custom-call(s32[8]{0:T(128)S(1)} %get-tuple-element.72.info, s32[2,8,128]{2,1,0:T(8,128)S(1)} %get-tuple-element.73.qrow, bf16[4,1024,128]{2,1,0:T(8,128)(2,1)S(1)} %get-tuple-element.74.qst, ...), custom_call_target="tpu_custom_call" | custom-call | flops 3000000000 | bytes 1000000 | tf_op jit(solution)/shard_map/pallas_call | solution.py:321
  42.7 2.7 %collective-permute-start.12 = (bf16[256,256]{1,0:T(8,128)(2,1)S(1)}, bf16[256,256]{1,0:T(8,128)(2,1)S(1)}, u32[]{:S(2)}, u32[]{:S(2)}) collective-permute-start(bf16[256,256]{1,0:T(8,128)(2,1)S(1)} %get-tuple-element.94), channel_id=1, source_target_pairs={{0,14},{1,15},{2,0},{3,1},{4,2},{5,3},{6,4},{7,5},{8,6},{9,7},{10,... | collective-permute-start | bytes 393224 | tf_op jit(solution)/shard_map/ppermute | solution.py:348
  45.3 3.4 %shard_map.82 = (bf16[256,512]{1,0:T(8,128)(2,1)S(1)}, bf16[256,512]{1,0:T(8,128)(2,1)S(1)}, f32[4,128,1024]{2,1,0:T(8,128)S(1)}) custom-call(s32[8]{0:T(128)S(1)} %get-tuple-element.72.info, s32[2,8,128]{2,1,0:T(8,128)S(1)} %get-tuple-element.73.qrow, bf16[4,1024,128]{2,1,0:T(8,128)(2,1)S(1)} %get-tuple-element.74.qst, ...), custom_call_target="tpu_custom_call" | custom-call | flops 5000000000 | bytes 1000000 | tf_op jit(solution)/shard_map/pallas_call | solution.py:321
  49.0 2.7 %collective-permute-start.14 = (bf16[256,512]{1,0:T(8,128)(2,1)S(1)}, bf16[256,512]{1,0:T(8,128)(2,1)S(1)}, u32[]{:S(2)}, u32[]{:S(2)}) collective-permute-start(bf16[256,512]{1,0:T(8,128)(2,1)S(1)} %pad_maximum_fusion.1), channel_id=1, source_target_pairs={{0,14},{1,15},{2,0},{3,1},{4,2},{5,3},{6,4},{7,5},{8,6},{9,7},{10,... | collective-permute-start | bytes 786440 | tf_op jit(solution)/shard_map/ppermute | solution.py:348
  51.7 4.0 %shard_map.83 = (bf16[256,512]{1,0:T(8,128)(2,1)S(1)}, bf16[256,512]{1,0:T(8,128)(2,1)S(1)}, f32[4,128,1024]{2,1,0:T(8,128)S(1)}) custom-call(s32[8]{0:T(128)S(1)} %get-tuple-element.72.info, s32[2,8,128]{2,1,0:T(8,128)S(1)} %get-tuple-element.73.qrow, bf16[4,1024,128]{2,1,0:T(8,128)(2,1)S(1)} %get-tuple-element.74.qst, ...), custom_call_target="tpu_custom_call" | custom-call | flops 5000000000 | bytes 1000000 | tf_op jit(solution)/shard_map/pallas_call | solution.py:321
  55.9 2.7 %collective-permute-start.16 = (bf16[256,512]{1,0:T(8,128)(2,1)S(1)}, bf16[256,512]{1,0:T(8,128)(2,1)S(1)}, u32[]{:S(2)}, u32[]{:S(2)}) collective-permute-start(bf16[256,512]{1,0:T(8,128)(2,1)S(1)} %add_convert_fusion.3), channel_id=1, source_target_pairs={{0,14},{1,15},{2,0},{3,1},{4,2},{5,3},{6,4},{7,5},{8,6},{9,7},{10,... | collective-permute-start | bytes 786440 | tf_op jit(solution)/shard_map/ppermute | solution.py:348
  58.6 3.4 %shard_map.84 = (bf16[256,512]{1,0:T(8,128)(2,1)S(1)}, bf16[256,512]{1,0:T(8,128)(2,1)S(1)}, f32[4,128,1024]{2,1,0:T(8,128)S(1)}) custom-call(s32[8]{0:T(128)S(1)} %get-tuple-element.72.info, s32[2,8,128]{2,1,0:T(8,128)S(1)} %get-tuple-element.73.qrow, bf16[4,1024,128]{2,1,0:T(8,128)(2,1)S(1)} %get-tuple-element.74.qst, ...), custom_call_target="tpu_custom_call" | custom-call | flops 5000000000 | bytes 1000000 | tf_op jit(solution)/shard_map/pallas_call | solution.py:321
  62.8 1.3 %collective-permute-start.17 = (bf16[256,512]{1,0:T(8,128)(2,1)S(1)}, bf16[256,512]{1,0:T(8,128)(2,1)S(1)}, u32[]{:S(2)}, u32[]{:S(2)}) collective-permute-start(bf16[256,512]{1,0:T(8,128)(2,1)S(1)} %add_convert_fusion.2), channel_id=1, source_target_pairs={{0,2},{1,3},{2,4},{3,5},{4,6},{5,7},{6,8},{7,9},{8,10},{9,11},{10,... | collective-permute-start | bytes 786440 | tf_op jit(solution)/shard_map/ppermute | solution.py:348
  64.1 1.5 %collective-permute-start.18 = (bf16[256,512]{1,0:T(8,128)(2,1)S(1)}, bf16[256,512]{1,0:T(8,128)(2,1)S(1)}, u32[]{:S(2)}, u32[]{:S(2)}) collective-permute-start(bf16[256,512]{1,0:T(8,128)(2,1)S(1)} %add_convert_fusion.1), channel_id=1, source_target_pairs={{0,14},{1,15},{2,0},{3,1},{4,2},{5,3},{6,4},{7,5},{8,6},{9,7},{10,... | collective-permute-start | bytes 786440 | tf_op jit(solution)/shard_map/ppermute | solution.py:348
  65.6 3.5 %shard_map.85 = (bf16[256,512]{1,0:T(8,128)(2,1)S(1)}, bf16[128,2048]{1,0:T(8,128)(2,1)S(1)}, bf16[128,2048]{1,0:T(8,128)(2,1)S(1)}) custom-call(s32[8]{0:T(128)S(1)} %get-tuple-element.72.info, s32[2,8,128]{2,1,0:T(8,128)S(1)} %get-tuple-element.73.qrow, bf16[4,1024,128]{2,1,0:T(8,128)(2,1)S(1)} %get-tuple-element.74.qst, ...), custom_call_target="tpu_custom_call" | custom-call | flops 5000000000 | bytes 1000000 | tf_op jit(solution)/shard_map/pallas_call | solution.py:321
  69.1 10.8 %collective-permute-start.19 = (bf16[128,2048]{1,0:T(8,128)(2,1)S(1)}, bf16[128,2048]{1,0:T(8,128)(2,1)S(1)}, u32[]{:S(2)}, u32[]{:S(2)}) collective-permute-start(bf16[128,2048]{1,0:T(8,128)(2,1)S(1)} %get-tuple-element.129), channel_id=1, source_target_pairs={{0,1},{1,0},{2,3},{3,2},{4,5},{5,4},{6,7},{7,6},{8,9},{9,8},{10,11... | collective-permute-start | bytes 1572872 | tf_op jit(solution)/shard_map/ppermute | solution.py:336
  82.7 1.3 %shard_map.86 = (bf16[128,512]{1,0:T(8,128)(2,1)}, bf16[128,512]{1,0:T(8,128)(2,1)}) custom-call(s32[2]{0:T(128)S(1)} %pad_add_fusion.place, bf16[256,512]{1,0:T(8,128)(2,1)S(1)} %add_convert_fusion.total, bf16[128,512]{1,0:T(8,128)(2,1)S(1)} %collective-permute-done.20.back), custom_call_target="tpu_custom_call" | custom-call | flops 3000000000 | bytes 1000000 | tf_op jit(solution)/shard_map/pallas_call | solution.py:321
  (56 shorter events, 8.6 us)
Async XLA Ops:
  1.6 1.7 %collective-permute-start = (bf16[128,512]{1,0:T(8,128)(2,1)S(1)}, bf16[128,512]{1,0:T(8,128)(2,1)S(1)}, u32[]{:S(2)}, u32[]{:S(2)}) collective-permute-start(bf16[128,512]{1,0:T(8,128)(2,1)S(1)} %pad_maximum_fusion.2), channel_id=1, source_target_pairs={{0,1},{1,0},{2,3},{3,2},{4,5},{5,4},{6,7},{7,6},{8,9},{9,8},{10,11... | collective-permute-start | bytes 393224 | tf_op jit(solution)/shard_map/ppermute | solution.py:336
  3.4 6.9 %collective-permute-start.1 = (bf16[128,4096]{1,0:T(8,128)(2,1)}, bf16[128,4096]{1,0:T(8,128)(2,1)S(1)}, u32[]{:S(2)}, u32[]{:S(2)}) collective-permute-start(bf16[128,4096]{1,0:T(8,128)(2,1)} %q_own.1), channel_id=1, source_target_pairs={{0,1},{1,0},{2,3},{3,2},{4,5},{5,4},{6,7},{7,6},{8,9},{9,8},{10,11... | collective-permute-start | bytes 3145736 | tf_op jit(solution)/shard_map/ppermute | solution.py:336
  3.7 6.5 %collective-permute-start.2 = (bf16[128,4096]{1,0:T(8,128)(2,1)}, bf16[128,4096]{1,0:T(8,128)(2,1)S(1)}, u32[]{:S(2)}, u32[]{:S(2)}) collective-permute-start(bf16[128,4096]{1,0:T(8,128)(2,1)} %do_own.1), channel_id=1, source_target_pairs={{0,1},{1,0},{2,3},{3,2},{4,5},{5,4},{6,7},{7,6},{8,9},{9,8},{10,11... | collective-permute-start | bytes 3145736 | tf_op jit(solution)/shard_map/ppermute | solution.py:336
  4.0 6.3 %copy-start = (bf16[128,4096]{1,0:T(8,128)(2,1)S(1)}, bf16[128,4096]{1,0:T(8,128)(2,1)}, u32[]{:S(2)}) copy-start(bf16[128,4096]{1,0:T(8,128)(2,1)} %q_own.1) | copy-start | bytes 3145732
  4.0 6.3 %copy-start.1 = (bf16[128,4096]{1,0:T(8,128)(2,1)S(1)}, bf16[128,4096]{1,0:T(8,128)(2,1)}, u32[]{:S(2)}) copy-start(bf16[128,4096]{1,0:T(8,128)(2,1)} %do_own.1) | copy-start | bytes 3145732
  4.0 6.3 %copy-start.2 = (s32[2048]{0:T(1024)S(1)}, s32[2048]{0:T(1024)}, u32[]{:S(2)}) copy-start(s32[2048]{0:T(1024)} %param.9) | copy-start | bytes 24580
  4.6 10.9 %collective-permute-start.3 = (bf16[256,512]{1,0:T(8,128)(2,1)S(1)}, bf16[256,512]{1,0:T(8,128)(2,1)S(1)}, u32[]{:S(2)}, u32[]{:S(2)}) collective-permute-start(bf16[256,512]{1,0:T(8,128)(2,1)S(1)} %get-tuple-element.76), channel_id=1, source_target_pairs={{0,2},{1,15},{2,4},{3,1},{4,6},{5,3},{6,8},{7,5},{8,10},{9,7},{10,... | collective-permute-start | bytes 786440 | tf_op jit(solution)/shard_map/ppermute | solution.py:343
  10.3 7.1 %collective-permute-start.4 = (bf16[256,512]{1,0:T(8,128)(2,1)S(1)}, bf16[256,512]{1,0:T(8,128)(2,1)S(1)}, u32[]{:S(2)}, u32[]{:S(2)}) collective-permute-start(bf16[256,512]{1,0:T(8,128)(2,1)S(1)} %get-tuple-element.77), channel_id=1, source_target_pairs={{0,14},{1,3},{2,0},{3,5},{4,2},{5,7},{6,4},{7,9},{8,6},{9,11},{10,... | collective-permute-start | bytes 786440 | tf_op jit(solution)/shard_map/ppermute | solution.py:343
  17.4 9.3 %collective-permute-start.5 = (bf16[256,512]{1,0:T(8,128)(2,1)S(1)}, bf16[256,512]{1,0:T(8,128)(2,1)S(1)}, u32[]{:S(2)}, u32[]{:S(2)}) collective-permute-start(bf16[256,512]{1,0:T(8,128)(2,1)S(1)} %get-tuple-element.81.up), channel_id=1, source_target_pairs={{0,2},{1,3},{2,4},{3,5},{4,6},{5,7},{6,8},{7,9},{8,10},{9,11},{10,... | collective-permute-start | bytes 786440 | tf_op jit(solution)/shard_map/ppermute | solution.py:348
  17.5 9.2 %collective-permute-start.6 = (bf16[256,512]{1,0:T(8,128)(2,1)S(1)}, bf16[256,512]{1,0:T(8,128)(2,1)S(1)}, u32[]{:S(2)}, u32[]{:S(2)}) collective-permute-start(bf16[256,512]{1,0:T(8,128)(2,1)S(1)} %get-tuple-element.82.down), channel_id=1, source_target_pairs={{0,14},{1,15},{2,0},{3,1},{4,2},{5,3},{6,4},{7,5},{8,6},{9,7},{10,... | collective-permute-start | bytes 786440 | tf_op jit(solution)/shard_map/ppermute | solution.py:348
  26.7 8.3 %collective-permute-start.7 = (bf16[256,512]{1,0:T(8,128)(2,1)S(1)}, bf16[256,512]{1,0:T(8,128)(2,1)S(1)}, u32[]{:S(2)}, u32[]{:S(2)}) collective-permute-start(bf16[256,512]{1,0:T(8,128)(2,1)S(1)} %collective-permute-done.5.up), channel_id=1, source_target_pairs={{0,2},{1,3},{2,4},{3,5},{4,6},{5,7},{6,8},{7,9},{8,10},{9,11},{10,... | collective-permute-start | bytes 786440 | tf_op jit(solution)/shard_map/ppermute | solution.py:348
  26.7 8.3 %collective-permute-start.8 = (bf16[256,512]{1,0:T(8,128)(2,1)S(1)}, bf16[256,512]{1,0:T(8,128)(2,1)S(1)}, u32[]{:S(2)}, u32[]{:S(2)}) collective-permute-start(bf16[256,512]{1,0:T(8,128)(2,1)S(1)} %collective-permute-done.6.down), channel_id=1, source_target_pairs={{0,14},{1,15},{2,0},{3,1},{4,2},{5,3},{6,4},{7,5},{8,6},{9,7},{10,... | collective-permute-start | bytes 786440 | tf_op jit(solution)/shard_map/ppermute | solution.py:348
  35.1 5.1 %collective-permute-start.9 = (bf16[256,256]{1,0:T(8,128)(2,1)S(1)}, bf16[256,256]{1,0:T(8,128)(2,1)S(1)}, u32[]{:S(2)}, u32[]{:S(2)}) collective-permute-start(bf16[256,256]{1,0:T(8,128)(2,1)S(1)} %slice.24), channel_id=1, source_target_pairs={{0,2},{1,3},{2,4},{3,5},{4,6},{5,7},{6,8},{7,9},{8,10},{9,11},{10,... | collective-permute-start | bytes 393224 | tf_op jit(solution)/shard_map/ppermute | solution.py:348
  35.2 5.0 %collective-permute-start.10 = (bf16[256,256]{1,0:T(8,128)(2,1)S(1)}, bf16[256,256]{1,0:T(8,128)(2,1)S(1)}, u32[]{:S(2)}, u32[]{:S(2)}) collective-permute-start(bf16[256,256]{1,0:T(8,128)(2,1)S(1)} %slice.25), channel_id=1, source_target_pairs={{0,14},{1,15},{2,0},{3,1},{4,2},{5,3},{6,4},{7,5},{8,6},{9,7},{10,... | collective-permute-start | bytes 393224 | tf_op jit(solution)/shard_map/ppermute | solution.py:348
  42.4 6.3 %collective-permute-start.11 = (bf16[256,256]{1,0:T(8,128)(2,1)S(1)}, bf16[256,256]{1,0:T(8,128)(2,1)S(1)}, u32[]{:S(2)}, u32[]{:S(2)}) collective-permute-start(bf16[256,256]{1,0:T(8,128)(2,1)S(1)} %get-tuple-element.93), channel_id=1, source_target_pairs={{0,2},{1,3},{2,4},{3,5},{4,6},{5,7},{6,8},{7,9},{8,10},{9,11},{10,... | collective-permute-start | bytes 393224 | tf_op jit(solution)/shard_map/ppermute | solution.py:348
  42.7 6.1 %collective-permute-start.12 = (bf16[256,256]{1,0:T(8,128)(2,1)S(1)}, bf16[256,256]{1,0:T(8,128)(2,1)S(1)}, u32[]{:S(2)}, u32[]{:S(2)}) collective-permute-start(bf16[256,256]{1,0:T(8,128)(2,1)S(1)} %get-tuple-element.94), channel_id=1, source_target_pairs={{0,14},{1,15},{2,0},{3,1},{4,2},{5,3},{6,4},{7,5},{8,6},{9,7},{10,... | collective-permute-start | bytes 393224 | tf_op jit(solution)/shard_map/ppermute | solution.py:348
  48.9 6.7 %collective-permute-start.13 = (bf16[256,512]{1,0:T(8,128)(2,1)S(1)}, bf16[256,512]{1,0:T(8,128)(2,1)S(1)}, u32[]{:S(2)}, u32[]{:S(2)}) collective-permute-start(bf16[256,512]{1,0:T(8,128)(2,1)S(1)} %pad_maximum_fusion), channel_id=1, source_target_pairs={{0,2},{1,3},{2,4},{3,5},{4,6},{5,7},{6,8},{7,9},{8,10},{9,11},{10,... | collective-permute-start | bytes 786440 | tf_op jit(solution)/shard_map/ppermute | solution.py:348
  49.0 6.7 %collective-permute-start.14 = (bf16[256,512]{1,0:T(8,128)(2,1)S(1)}, bf16[256,512]{1,0:T(8,128)(2,1)S(1)}, u32[]{:S(2)}, u32[]{:S(2)}) collective-permute-start(bf16[256,512]{1,0:T(8,128)(2,1)S(1)} %pad_maximum_fusion.1), channel_id=1, source_target_pairs={{0,14},{1,15},{2,0},{3,1},{4,2},{5,3},{6,4},{7,5},{8,6},{9,7},{10,... | collective-permute-start | bytes 786440 | tf_op jit(solution)/shard_map/ppermute | solution.py:348
  55.8 6.5 %collective-permute-start.15 = (bf16[256,512]{1,0:T(8,128)(2,1)S(1)}, bf16[256,512]{1,0:T(8,128)(2,1)S(1)}, u32[]{:S(2)}, u32[]{:S(2)}) collective-permute-start(bf16[256,512]{1,0:T(8,128)(2,1)S(1)} %add_convert_fusion.4), channel_id=1, source_target_pairs={{0,2},{1,3},{2,4},{3,5},{4,6},{5,7},{6,8},{7,9},{8,10},{9,11},{10,... | collective-permute-start | bytes 786440 | tf_op jit(solution)/shard_map/ppermute | solution.py:348
  55.9 6.8 %collective-permute-start.16 = (bf16[256,512]{1,0:T(8,128)(2,1)S(1)}, bf16[256,512]{1,0:T(8,128)(2,1)S(1)}, u32[]{:S(2)}, u32[]{:S(2)}) collective-permute-start(bf16[256,512]{1,0:T(8,128)(2,1)S(1)} %add_convert_fusion.3), channel_id=1, source_target_pairs={{0,14},{1,15},{2,0},{3,1},{4,2},{5,3},{6,4},{7,5},{8,6},{9,7},{10,... | collective-permute-start | bytes 786440 | tf_op jit(solution)/shard_map/ppermute | solution.py:348
  62.8 17.1 %collective-permute-start.17 = (bf16[256,512]{1,0:T(8,128)(2,1)S(1)}, bf16[256,512]{1,0:T(8,128)(2,1)S(1)}, u32[]{:S(2)}, u32[]{:S(2)}) collective-permute-start(bf16[256,512]{1,0:T(8,128)(2,1)S(1)} %add_convert_fusion.2), channel_id=1, source_target_pairs={{0,2},{1,3},{2,4},{3,5},{4,6},{5,7},{6,8},{7,9},{8,10},{9,11},{10,... | collective-permute-start | bytes 786440 | tf_op jit(solution)/shard_map/ppermute | solution.py:348
  64.1 15.8 %collective-permute-start.18 = (bf16[256,512]{1,0:T(8,128)(2,1)S(1)}, bf16[256,512]{1,0:T(8,128)(2,1)S(1)}, u32[]{:S(2)}, u32[]{:S(2)}) collective-permute-start(bf16[256,512]{1,0:T(8,128)(2,1)S(1)} %add_convert_fusion.1), channel_id=1, source_target_pairs={{0,14},{1,15},{2,0},{3,1},{4,2},{5,3},{6,4},{7,5},{8,6},{9,7},{10,... | collective-permute-start | bytes 786440 | tf_op jit(solution)/shard_map/ppermute | solution.py:348
  69.1 12.3 %collective-permute-start.19 = (bf16[128,2048]{1,0:T(8,128)(2,1)S(1)}, bf16[128,2048]{1,0:T(8,128)(2,1)S(1)}, u32[]{:S(2)}, u32[]{:S(2)}) collective-permute-start(bf16[128,2048]{1,0:T(8,128)(2,1)S(1)} %get-tuple-element.129), channel_id=1, source_target_pairs={{0,1},{1,0},{2,3},{3,2},{4,5},{5,4},{6,7},{7,6},{8,9},{9,8},{10,11... | collective-permute-start | bytes 1572872 | tf_op jit(solution)/shard_map/ppermute | solution.py:336
  80.0 2.6 %collective-permute-start.20 = (bf16[128,512]{1,0:T(8,128)(2,1)S(1)}, bf16[128,512]{1,0:T(8,128)(2,1)S(1)}, u32[]{:S(2)}, u32[]{:S(2)}) collective-permute-start(bf16[128,512]{1,0:T(8,128)(2,1)S(1)} %pad_maximum_fusion.4), channel_id=1, source_target_pairs={{0,1},{1,0},{2,3},{3,2},{4,5},{5,4},{6,7},{7,6},{8,9},{9,8},{10,11... | collective-permute-start | bytes 393224 | tf_op jit(solution)/shard_map/ppermute | solution.py:336
